TPU v7x, 512 devices: a whole 4x8x8 slice. The times are simulated.
512 devices in a mesh: wide: 8 (over x, z_hi), narrow: 64 (over z_lo, y, core).
Axes of the slice: x: 4, y: 8, z: 8 (z_hi: 2, z_lo: 4; z = z_hi * 4 + z_lo), core: 2. Of those that a mesh axis runs over, the one named last changes fastest.
Arguments:
- queries: bfloat16 [262144, 512], P(('wide', 'narrow')), as said below
- targets: int32 [262144], P(('wide', 'narrow')), may hold values from 0 to 1535
- lengths: int32 [1024], P(('wide', 'narrow')), may hold values from 1 to 256, as said below
- contrast_items: bfloat16 [1536, 512], P(('wide', 'narrow')), as said below
Outputs:
- query_grads: bfloat16 [262144, 512], P(('wide', 'narrow'))
- item_grads: float32 [1536, 512], P(('wide', 'narrow'))
- query_loss: float32 [262144], P(('wide', 'narrow'))
Inputs may be any that keep to these rules, and one draw needn't show every extreme that they name: `lengths`: each sequence's count of valid positions; some sequence has all 256 valid. `contrast_items`: rows of roughly unit length. `queries`: entries within -2 and 2.
All inputs are finite; a program needn't handle non-finite values.
Results may differ from a plain program's by a relative error of at most 0.0034.
Values may be sent and summed in bfloat16 or wider, within the bound.
A program may use at most 64 MiB of HBM per device.

v0:
```python
import jax
import jax.numpy as jnp
from jax import lax
from jax.sharding import PartitionSpec as P

SEQ_LEN = 256


sharpness_factor = 20.0


def passed_along(value, axis, steps):
    count = lax.axis_size(axis)
    pairs = [(source, (source + steps) % count) for source in range(count)]
    return lax.ppermute(value, axis, pairs)


def block_scores(queries, pool_block):
    return (
        lax.dot_general(
            queries, pool_block, (((1,), (1,)), ((), ())), preferred_element_type=jnp.float32
        )
        * sharpness_factor
    )


def target_hits(targets, anchor, breadth):
    offset = targets - anchor * breadth
    return (offset[:, None] == jnp.arange(breadth, dtype=jnp.int32)[None, :]).astype(jnp.float32)


def body(queries, targets, lengths, contrast_items):
    request_embeds = queries.shape[0]
    width = queries.shape[1]
    owned = contrast_items.shape[0]
    cycle_size = lax.axis_size("wide")
    wide_place = lax.axis_index("wide")
    position = jnp.arange(request_embeds, dtype=jnp.int32) % SEQ_LEN
    validity_mask = (position < jnp.repeat(lengths, SEQ_LEN)).astype(jnp.float32)
    group_block = lax.all_gather(contrast_items, "narrow", axis=0, tiled=True)
    breadth = group_block.shape[0]
    running = jnp.full((request_embeds,), -1e30, jnp.float32)
    exp_total = jnp.zeros((request_embeds,), jnp.float32)
    target_score = jnp.zeros((request_embeds,), jnp.float32)
    visiting = group_block
    for turn in range(cycle_size):
        anchor = (wide_place - turn) % cycle_size
        affinity_matrix = block_scores(queries, visiting)
        positive_indicator = target_hits(targets, anchor, breadth)
        target_score = target_score + jnp.sum(positive_indicator * affinity_matrix, axis=1)
        new_max = jnp.maximum(running, jnp.max(affinity_matrix, axis=1))
        exp_total = exp_total * jnp.exp(running - new_max) + jnp.sum(
            jnp.exp(affinity_matrix - new_max[:, None]), axis=1
        )
        running = new_max
        if turn + 1 < cycle_size:
            visiting = passed_along(visiting, "wide", 1)
    normalizer_term = running + jnp.log(exp_total)
    query_loss = validity_mask * (normalizer_term - target_score)
    query_total = jnp.zeros((request_embeds, width), jnp.float32)
    collected = jnp.zeros((cycle_size * owned, width), jnp.float32)
    visiting = group_block
    for turn in range(cycle_size):
        anchor = (wide_place - turn) % cycle_size
        affinity_matrix = block_scores(queries, visiting)
        positive_indicator = target_hits(targets, anchor, breadth)
        score_derivative = (
            validity_mask[:, None]
            * (jnp.exp(affinity_matrix - normalizer_term[:, None]) - positive_indicator)
            * sharpness_factor
        ).astype(jnp.bfloat16)
        query_total = query_total + jnp.dot(
            score_derivative, visiting, preferred_element_type=jnp.float32
        )

        def item_terms(start, count, score_derivative=score_derivative):
            return lax.dot_general(
                score_derivative,
                queries,
                (((0,), (0,)), ((), ())),
                preferred_element_type=jnp.float32,
            )

        summed_piece = lax.psum_scatter(
            item_terms(jnp.int32(0), owned * lax.axis_size("narrow")),
            "narrow",
            scatter_dimension=0,
            tiled=True,
        )
        collected = lax.dynamic_update_slice_in_dim(collected, summed_piece, anchor * owned, 0)
        if turn + 1 < cycle_size:
            visiting = passed_along(visiting, "wide", 1)
    item_grads = lax.psum_scatter(collected, "wide", scatter_dimension=0, tiled=True)
    return (query_total.astype(jnp.bfloat16), item_grads, query_loss)


def solution(mesh):
    placed = (
        P(("wide", "narrow"), None),
        P(("wide", "narrow")),
        P(("wide", "narrow")),
        P(("wide", "narrow"), None),
    )
    return jax.shard_map(
        body,
        mesh=mesh,
        in_specs=placed,
        out_specs=(P(("wide", "narrow"), None), P(("wide", "narrow"), None), P(("wide", "narrow"))),
        check_vma=False,
    )
```

profile of v0, /device:TPU:1, one launch (start us, length us, event | category | flops | bytes accessed | tf_op | source)
XLA Modules:
  0.0 815.9 jit_solution(14745832452093103460)
XLA Ops:
  7.2 85.2 %all-gather = bf16[64,3,512]{2,1,0:T(4,128)(2,1)S(1)} all-gather(bf16[1,3,512]{2,1,0:T(4,128)(2,1)} %bitcast.39), channel_id=1, replica_groups=mesh['wide'=8,'narrow'=64] {'narrow'}, dimensions={0}, use_global_device_ids=true | all-gather | bytes 199680 | tf_op jit(solution)/shard_map/all_gather | solution.py:40
  92.6 7.8 collective-permute-start
  100.5 1.1 fusion.25
  103.0 9.2 %collective-permute-done = bf16[192,512]{1,0:T(8,128)(2,1)S(1)} collective-permute-done((bf16[192,512]{1,0:T(8,128)(2,1)S(1)}, bf16[192,512]{1,0:T(8,128)(2,1)S(1)}, u32[]{:S(2)}, u32[]{:S(2)}) %collective-permute-start) | collective-permute-done | bytes 196640 | tf_op jit(solution)/shard_map/ppermute | solution.py:15
  112.2 1.9 collective-permute-start.1
  114.5 11.8 %collective-permute-done.1 = bf16[192,512]{1,0:T(8,128)(2,1)S(1)} collective-permute-done((bf16[192,512]{1,0:T(8,128)(2,1)S(1)}, bf16[192,512]{1,0:T(8,128)(2,1)S(1)}, u32[]{:S(2)}, u32[]{:S(2)}) %collective-permute-start.1) | collective-permute-done | bytes 196640 | tf_op jit(solution)/shard_map/ppermute | solution.py:15
  126.3 1.9 collective-permute-start.2
  128.5 10.7 %collective-permute-done.2 = bf16[192,512]{1,0:T(8,128)(2,1)S(1)} collective-permute-done((bf16[192,512]{1,0:T(8,128)(2,1)S(1)}, bf16[192,512]{1,0:T(8,128)(2,1)S(1)}, u32[]{:S(2)}, u32[]{:S(2)}) %collective-permute-start.2) | collective-permute-done | bytes 196640 | tf_op jit(solution)/shard_map/ppermute | solution.py:15
  139.3 1.9 collective-permute-start.3
  141.5 10.1 %collective-permute-done.3 = bf16[192,512]{1,0:T(8,128)(2,1)S(1)} collective-permute-done((bf16[192,512]{1,0:T(8,128)(2,1)S(1)}, bf16[192,512]{1,0:T(8,128)(2,1)S(1)}, u32[]{:S(2)}, u32[]{:S(2)}) %collective-permute-start.3) | collective-permute-done | bytes 196640 | tf_op jit(solution)/shard_map/ppermute | solution.py:15
  151.7 1.9 collective-permute-start.4
  154.0 10.2 %collective-permute-done.4 = bf16[192,512]{1,0:T(8,128)(2,1)S(1)} collective-permute-done((bf16[192,512]{1,0:T(8,128)(2,1)S(1)}, bf16[192,512]{1,0:T(8,128)(2,1)S(1)}, u32[]{:S(2)}, u32[]{:S(2)}) %collective-permute-start.4) | collective-permute-done | bytes 196640 | tf_op jit(solution)/shard_map/ppermute | solution.py:15
  164.1 1.9 collective-permute-start.5
  166.4 10.2 %collective-permute-done.5 = bf16[192,512]{1,0:T(8,128)(2,1)S(1)} collective-permute-done((bf16[192,512]{1,0:T(8,128)(2,1)S(1)}, bf16[192,512]{1,0:T(8,128)(2,1)S(1)}, u32[]{:S(2)}, u32[]{:S(2)}) %collective-permute-start.5) | collective-permute-done | bytes 196640 | tf_op jit(solution)/shard_map/ppermute | solution.py:15
  176.5 1.9 collective-permute-start.6
  178.8 10.2 %collective-permute-done.6 = bf16[192,512]{1,0:T(8,128)(2,1)S(1)} collective-permute-done((bf16[192,512]{1,0:T(8,128)(2,1)S(1)}, bf16[192,512]{1,0:T(8,128)(2,1)S(1)}, u32[]{:S(2)}, u32[]{:S(2)}) %collective-permute-start.6) | collective-permute-done | bytes 196640 | tf_op jit(solution)/shard_map/ppermute | solution.py:15
  190.3 0.8 copy-done.1
  191.9 1.0 fusion.6
  192.9 1.0 fusion.8
  194.0 1.0 fusion.9
  195.0 1.0 fusion.10
  196.0 1.0 fusion.11
  197.1 1.0 fusion.12
  198.1 1.1 fusion.13
  199.2 1.0 fusion.14
  200.3 1.3 dynamic-slice
  201.6 1.3 dynamic-slice.16
  204.2 1.4 fusion.7
  211.2 1.2 fusion
  212.3 543.2 %all-reduce.12.cloned.1.call-done = (f32[192,512]{1,0:T(8,128)}, f32[192,512]{1,0:T(8,128)}, f32[192,512]{1,0:T(8,128)}, f32[192,512]{1,0:T(8,128)}, f32[192,512...) async-done(((f32[192,512]{1,0:T(8,128)}, f32[192,512]{1,0:T(8,128)}, f32[192,512]{1,0:T(8,128)}, f32[192,512]{1,0:T(8,128)}, ...) | async-done | bytes 3145744
  755.6 0.8 constant_dynamic-slice_fusion.8
  763.3 45.2 %all-reduce.8 = f32[24,512]{1,0:T(8,128)S(1)} all-reduce(f32[24,512]{1,0:T(8,128)S(1)} %dynamic_update_slice.31), channel_id=10, replica_groups=mesh['wide'=8,'narrow'=64] {'wide'}, use_global_device_ids=true, to_apply=%region_24.25.clone | all-reduce | flops 12288 | bytes 98304
  (78 shorter events, 18.8 us)
Async XLA Ops:
  7.2 93.4 %copy-start = (bf16[512,512]{1,0:T(8,128)(2,1)S(1)}, bf16[512,512]{1,0:T(8,128)(2,1)}, u32[]{:S(2)}) copy-start(bf16[512,512]{1,0:T(8,128)(2,1)} %param.4) | copy-start | bytes 1572868
  7.2 748.4 %all-reduce.12.cloned.1.call-start = ((), (), s32[]{:S(2)}) async-start(), calls=%async_computation | async-start | bytes 6291456
  92.6 19.6 %collective-permute-start = (bf16[192,512]{1,0:T(8,128)(2,1)S(1)}, bf16[192,512]{1,0:T(8,128)(2,1)S(1)}, u32[]{:S(2)}, u32[]{:S(2)}) collective-permute-start(bf16[192,512]{1,0:T(8,128)(2,1)S(1)} %reshape.180), channel_id=1, source_target_pairs={{0,64},{64,128},{128,192},{192,256},{256,320},{320,384},{384,448},... | collective-permute-start | bytes 589832 | tf_op jit(solution)/shard_map/ppermute | solution.py:15
  101.6 0.7 copy-start.17
  102.3 0.7 copy-start.16
  112.2 2.3 copy-start.2
  112.2 14.0 %collective-permute-start.1 = (bf16[192,512]{1,0:T(8,128)(2,1)S(1)}, bf16[192,512]{1,0:T(8,128)(2,1)S(1)}, u32[]{:S(2)}, u32[]{:S(2)}) collective-permute-start(bf16[192,512]{1,0:T(8,128)(2,1)S(1)} %collective-permute-done), channel_id=1, source_target_pairs={{0,64},{64,128},{128,192},{192,256},{256,320},{320,384},{384,448},... | collective-permute-start | bytes 589832 | tf_op jit(solution)/shard_map/ppermute | solution.py:15
  126.2 2.3 copy-start.4
  126.3 13.0 %collective-permute-start.2 = (bf16[192,512]{1,0:T(8,128)(2,1)S(1)}, bf16[192,512]{1,0:T(8,128)(2,1)S(1)}, u32[]{:S(2)}, u32[]{:S(2)}) collective-permute-start(bf16[192,512]{1,0:T(8,128)(2,1)S(1)} %collective-permute-done.1), channel_id=1, source_target_pairs={{0,64},{64,128},{128,192},{192,256},{256,320},{320,384},{384,448},... | collective-permute-start | bytes 589832 | tf_op jit(solution)/shard_map/ppermute | solution.py:15
  139.3 2.3 copy-start.6
  139.3 12.4 %collective-permute-start.3 = (bf16[192,512]{1,0:T(8,128)(2,1)S(1)}, bf16[192,512]{1,0:T(8,128)(2,1)S(1)}, u32[]{:S(2)}, u32[]{:S(2)}) collective-permute-start(bf16[192,512]{1,0:T(8,128)(2,1)S(1)} %collective-permute-done.2), channel_id=1, source_target_pairs={{0,64},{64,128},{128,192},{192,256},{256,320},{320,384},{384,448},... | collective-permute-start | bytes 589832 | tf_op jit(solution)/shard_map/ppermute | solution.py:15
  151.7 2.3 copy-start.8
  151.7 12.4 %collective-permute-start.4 = (bf16[192,512]{1,0:T(8,128)(2,1)S(1)}, bf16[192,512]{1,0:T(8,128)(2,1)S(1)}, u32[]{:S(2)}, u32[]{:S(2)}) collective-permute-start(bf16[192,512]{1,0:T(8,128)(2,1)S(1)} %collective-permute-done.3), channel_id=1, source_target_pairs={{0,64},{64,128},{128,192},{192,256},{256,320},{320,384},{384,448},... | collective-permute-start | bytes 589832 | tf_op jit(solution)/shard_map/ppermute | solution.py:15
  164.1 2.3 copy-start.10
  164.1 12.4 %collective-permute-start.5 = (bf16[192,512]{1,0:T(8,128)(2,1)S(1)}, bf16[192,512]{1,0:T(8,128)(2,1)S(1)}, u32[]{:S(2)}, u32[]{:S(2)}) collective-permute-start(bf16[192,512]{1,0:T(8,128)(2,1)S(1)} %collective-permute-done.4), channel_id=1, source_target_pairs={{0,64},{64,128},{128,192},{192,256},{256,320},{320,384},{384,448},... | collective-permute-start | bytes 589832 | tf_op jit(solution)/shard_map/ppermute | solution.py:15
  176.5 2.3 copy-start.12
  176.5 12.4 %collective-permute-start.6 = (bf16[192,512]{1,0:T(8,128)(2,1)S(1)}, bf16[192,512]{1,0:T(8,128)(2,1)S(1)}, u32[]{:S(2)}, u32[]{:S(2)}) collective-permute-start(bf16[192,512]{1,0:T(8,128)(2,1)S(1)} %collective-permute-done.5), channel_id=1, source_target_pairs={{0,64},{64,128},{128,192},{192,256},{256,320},{320,384},{384,448},... | collective-permute-start | bytes 589832 | tf_op jit(solution)/shard_map/ppermute | solution.py:15
  189.0 0.7 copy-start.14
  190.1 1.0 copy-start.1
  204.2 1.4 copy-start.3
  205.6 0.9 copy-start.5
  206.5 0.9 copy-start.7
  207.5 0.9 copy-start.9
  208.4 0.9 copy-start.11
  209.3 0.9 copy-start.13
  210.2 0.9 copy-start.15
Sparse Core Ops, SparseCore 0:
  200.3 555.1 all-reduce.11
where the time goes:
time: 824 us; the launch traced here: 816 us
  waiting for transfers between devices  616 us (75%)
  blocking collectives  130 us (16%)
  starting transfers between devices  19.3 us (2%)
  local copies, waits for them, and re-layouts  16.9 us (2%)
  matrix products  16.4 us (2%)
  between operations  15.8 us (2%)
    unnamed x2, waiting for transfers between devices  543 us
    all_gather x1, blocking collectives, body(): group_block = lax.all_gather(contrast_items, 'narrow', axis=0, tiled=True)  85.2 us
    ppermute x7, waiting for transfers between devices, passed_along(): return lax.ppermute(value, axis, pairs)  72.3 us
    unnamed x1, blocking collectives  45.2 us
    ppermute x7, starting transfers between devices, passed_along(): return lax.ppermute(value, axis, pairs)  19.3 us
  transfers between devices with their start and end apart: 8, of which 8 were waited for; matrix products, arithmetic and copies ran while one was open for 1% of the time, Pallas kernels for 0%

commit v1 on v0

v1 whole, which is shorter than its diff:
```python
import functools

import jax
import jax.numpy as jnp
from jax import lax
from jax.experimental import pallas as pl
from jax.experimental.pallas import tpu as pltpu
from jax.sharding import PartitionSpec as P

MESH = pl.DeviceIdType.MESH
SEQ_LEN = 256
SHARPNESS = 20.0
LOG2E = 1.4426950408889634
ZHI = 2
OWNED = 3
BLK = 16


def kernel(X, Y, Z, q_hbm, tgt_ref, len_ref, it_ref, qg_ref, ig_ref, loss_ref,
           q_all, info, stat, pool, pack, blk, land, scores, grads, out_items, in_items,
           acc, pieces, land2, qpart, qland,
           q_sem, pair_ssem, pair_rsem, s1_ssem, s1_rsem, s2_ssem, s2_rsem,
           r1_ssem, r1_rsem, r2_ssem, r2_rsem):
    zlo = Z // ZHI
    wide, narrow = lax.axis_index("wide"), lax.axis_index("narrow")
    x, c = wide // ZHI, narrow % 2
    y, z = (narrow // 2) % Y, (wide % ZHI) * zlo + narrow // (2 * Y)
    qd, width = q_hbm.shape
    chunks = width // 128
    slab = Y * Z * OWNED
    half = X * slab // 2
    yrows, zrows = half // Y, half // Z
    items = X * slab
    even = x % 2 == 0

    def dev(px, py, pz, pc):
        return (px * ZHI + pz // zlo, ((pz % zlo) * Y + py) * 2 + pc)

    def yz_peer(i):
        return (y + i // Z) % Y, (z + i % Z) % Z

    def xz_peer(i):
        return (x + i // Z) % X, (z + i % Z) % Z

    def xy_peer(i):
        return (x + i // Y) % X, (y + i % Y) % Y

    def remote(src, dst, ssem, rsem, to):
        return pltpu.make_async_remote_copy(
            src_ref=src, dst_ref=dst, send_sem=ssem, recv_sem=rsem, device_id=to, device_id_type=MESH)

    def bytes_of(ref, sem):
        return pltpu.make_async_copy(ref, ref, sem)

    def loop(lo, hi, f):
        def step(i, carry):
            f(i)
            return carry
        lax.fori_loop(lo, hi, step, 0)

    load_q = pltpu.make_async_copy(q_hbm, q_all.at[c], q_sem)
    load_q.start()

    barrier = pltpu.get_barrier_semaphore()
    partner = dev(x, y, z, 1 - c)

    def greet(to):
        pl.semaphore_signal(barrier, inc=1, device_id=to, device_id_type=MESH)

    greet(partner)

    @pl.when(c == 0)
    def _():
        def one(i):
            py, pz = yz_peer(i)
            greet(dev(x, py, pz, 0))
        loop(1, Y * Z, one)
        loop(1, X, lambda i: greet(dev((x + i) % X, y, z, 0)))

    @pl.when(c == 1)
    def _():
        def one(i):
            px, pz = xz_peer(i)
            greet(dev(px, y, pz, 1))
        loop(1, X * Z, one)

        def two(i):
            px, py = xy_peer(i)
            greet(dev(px, py, z, 1))
        loop(1, X * Y, two)

    own = it_ref[...].astype(jnp.float32)
    pack[pl.ds(0, BLK), :] = jnp.zeros((BLK, 128), jnp.float32)
    for a in range(chunks):
        pack[pl.ds(a * OWNED, OWNED), :] = own[:, a * 128:(a + 1) * 128]
    blk[...] = pack[pl.ds(0, BLK), :].astype(jnp.bfloat16)

    pos = lax.broadcasted_iota(jnp.int32, (1, qd), 1)
    live = jnp.where(pos < SEQ_LEN, (pos < len_ref[0]).astype(jnp.float32),
                     (pos - SEQ_LEN < len_ref[1]).astype(jnp.float32))
    info[c, pl.ds(0, 1), :] = tgt_ref[...].astype(jnp.float32)
    info[c, pl.ds(1, 1), :] = live
    info[c, pl.ds(2, 6), :] = jnp.zeros((6, qd), jnp.float32)
    load_q.wait()

    @pl.when(c == 0)
    def _():
        pl.semaphore_wait(barrier, Y * Z - 1 + X - 1 + 1)

    @pl.when(c == 1)
    def _():
        pl.semaphore_wait(barrier, X * Z - 1 + X * Y - 1 + 1)

    def rows(i):
        return pl.ds(pl.multiple_of(i * BLK, BLK), BLK)

    s1_copies = []

    @pl.when(c == 0)
    def _():
        me = y * Z + z
        land[rows(me), :] = blk[...]

        def one(i):
            py, pz = yz_peer(i)
            remote(blk, land.at[rows(me)], s1_ssem, s1_rsem, dev(x, py, pz, 0)).start()
        loop(1, Y * Z, one)

    @pl.when(jnp.logical_and(c == 1, even))
    def _():
        me = (x // 2) * Z + z
        land[rows(me), :] = blk[...]

        def one(i):
            px, pz = xz_peer(i)
            remote(blk, land.at[rows(me)], s1_ssem, s1_rsem, dev(px, y, pz, 1)).start()
        loop(1, X * Z, one)

    @pl.when(jnp.logical_and(c == 1, jnp.logical_not(even)))
    def _():
        me = X // 2 * Z + (x // 2) * Y + y
        land[rows(me), :] = blk[...]

        def one(i):
            px, py = xy_peer(i)
            remote(blk, land.at[rows(me)], s1_ssem, s1_rsem, dev(px, py, z, 1)).start()
        loop(1, X * Y, one)

    q_copy = remote(q_all.at[c], q_all.at[c], pair_ssem.at[0], pair_rsem.at[0], partner)
    q_copy.start()
    info_copy = remote(info.at[c], info.at[c], pair_ssem.at[1], pair_rsem.at[1], partner)
    info_copy.start()

    @pl.when(c == 0)
    def _():
        bytes_of(land.at[pl.ds(0, (Y * Z - 1) * BLK)], s1_rsem).wait()

    @pl.when(c == 1)
    def _():
        bytes_of(land.at[pl.ds(0, (X * Z - 1) * BLK)], s1_rsem).wait()

    def unpack(first, owners, base):
        n = owners * BLK
        pack[pl.ds(0, n), :] = land[pl.ds(first * BLK, n), :].astype(jnp.float32)
        for r in range(OWNED):
            for a in range(chunks):
                piece = pack[pl.ds(a * OWNED + r, owners, stride=BLK), :]
                at = base + r * owners
                pool[pl.ds(pl.multiple_of(at, 16), owners), a * 128:(a + 1) * 128] = piece.astype(jnp.bfloat16)

    xz_own, xy_own = X // 2 * Z, X // 2 * Y

    def slab0(px):
        return pl.ds(pl.multiple_of(px * slab, 16), slab)

    def slab_y(py):
        return pl.ds(pl.multiple_of(py * yrows, 16), yrows)

    def slab_z(pz):
        return pl.ds(pl.multiple_of(half + pz * zrows, 16), zrows)

    @pl.when(c == 0)
    def _():
        unpack(0, Y * Z, x * slab)

        def one(i):
            px = (x + i) % X
            remote(pool.at[slab0(x)], pool.at[slab0(x)], s2_ssem, s2_rsem, dev(px, y, z, 0)).start()
        loop(1, X, one)
        bytes_of(pool.at[pl.ds(0, (X - 1) * slab)], s2_rsem).wait()

    @pl.when(c == 1)
    def _():
        unpack(0, xz_own, y * yrows)

        def one(i):
            remote(pool.at[slab_y(y)], pool.at[slab_y(y)], s2_ssem, s2_rsem, dev(x, (y + i) % Y, z, 1)).start()
        loop(1, Y, one)
        unpack(xz_own, xy_own, half + z * zrows)

        def two(i):
            remote(pool.at[slab_z(z)], pool.at[slab_z(z)], s2_ssem, s2_rsem, dev(x, y, (z + i) % Z, 1)).start()
        loop(1, Z, two)
        bytes_of(pool.at[pl.ds(0, (Y - 1) * yrows + (Z - 1) * zrows)], s2_rsem).wait()

    q_copy.wait()
    info_copy.wait()

    def local_row(h):
        t = info[h, pl.ds(0, 1), :].astype(jnp.int32)
        o = (t * 21846) >> 16
        r = t - o * OWNED
        w, n = o // (zlo * Y * 2), o % (zlo * Y * 2)
        tx, tc = w // ZHI, n % 2
        ty, tz = (n // 2) % Y, (w % ZHI) * zlo + n // (2 * Y)
        on0 = tx * slab + r * (Y * Z) + ty * Z + tz
        on1 = jnp.where(tx % 2 == 0, ty * yrows + r * xz_own + (tx // 2) * Z + tz,
                        half + tz * zrows + r * xy_own + (tx // 2) * Y + ty)
        return jnp.where(tc == c, jnp.where(tc == 0, on0, on1), -1)

    tile = items // 3
    step = max(8, items // 12)
    fold = functools.partial(jnp.reshape, shape=(step // 8, 8, qd))
    row_iota = lax.broadcasted_iota(jnp.int32, (step, qd), 0)
    K = SHARPNESS * LOG2E

    def first_pass(h):
        m8 = jnp.full((8, qd), -3e38, jnp.float32)
        for i in range(3):
            s = lax.dot_general(pool[pl.ds(i * tile, tile), :], q_all[h], (((1,), (1,)), ((), ())),
                                preferred_element_type=jnp.float32)
            scores[h, pl.ds(i * tile, tile), :] = s
            m8 = jnp.maximum(m8, jnp.max(s.reshape(tile // 8, 8, qd), axis=0))
        m = jnp.max(m8, axis=0, keepdims=True)
        target = local_row(h)

        def body(i, carry):
            l8, t8 = carry
            at = pl.ds(pl.multiple_of(i * step, 8), step)
            s = scores[h, at, :]
            hit = row_iota == target - i * step
            e = jnp.exp2((s - m) * K)
            scores[h, at, :] = e
            return l8 + jnp.sum(fold(e), axis=0), t8 + jnp.sum(fold(jnp.where(hit, s, 0.0)), axis=0)

        zero = jnp.zeros((8, qd), jnp.float32)
        l8, t8 = lax.fori_loop(0, items // step, body, (zero, zero))
        stat[0, h, pl.ds(0, 1), :] = m
        stat[0, h, pl.ds(1, 1), :] = jnp.sum(l8, axis=0, keepdims=True)
        stat[0, h, pl.ds(2, 1), :] = jnp.sum(t8, axis=0, keepdims=True)
        stat[0, h, pl.ds(3, 5), :] = jnp.zeros((5, qd), jnp.float32)
        remote(stat.at[0, h], stat.at[1, h], pair_ssem.at[2 + h], pair_rsem.at[2 + h], partner).start()

    loop(0, 2, first_pass)

    def second_pass(h):
        remote(stat.at[0, h], stat.at[1, h], pair_ssem.at[2 + h], pair_rsem.at[2 + h], partner).wait()
        m, l, t = (stat[0, h, pl.ds(k, 1), :] for k in range(3))
        m2, l2, t2 = (stat[1, h, pl.ds(k, 1), :] for k in range(3))
        top = jnp.maximum(m, m2)
        mine = jnp.exp2((m - top) * K)
        total = l * mine + l2 * jnp.exp2((m2 - top) * K)
        valid = info[h, pl.ds(1, 1), :]
        weight = SHARPNESS * valid
        factor = weight * mine / total
        target = local_row(h)

        @pl.when(h == c)
        def _():
            loss_ref[...] = valid * (SHARPNESS * (top - (t + t2)) + jnp.log(total))

        def body(i):
            at = pl.ds(pl.multiple_of(i * step, 16), step)
            hit = row_iota == target - i * step
            g = scores[h, at, :] * factor - jnp.where(hit, weight, 0.0)
            grads[h, at, :] = g.astype(jnp.bfloat16)
        loop(0, items // step, body)

    loop(0, 2, second_pass)

    def item_tile(i):
        px = (x + 1 + i) % X
        at = slab0(px)
        g = jnp.dot(grads[0, at, :], q_all[0], preferred_element_type=jnp.float32)
        g = g + jnp.dot(grads[1, at, :], q_all[1], preferred_element_type=jnp.float32)
        out_items[at, :] = g.astype(jnp.bfloat16)

        @pl.when(jnp.logical_and(c == 0, px != x))
        def _():
            remote(out_items.at[at], in_items.at[slab0(x)], r1_ssem, r1_rsem, dev(px, y, z, 0)).start()

    loop(0, X, item_tile)

    @pl.when(c == 1)
    def _():
        def one(i):
            py = (y + i) % Y
            remote(out_items.at[slab_y(py)], in_items.at[slab_y(y)], r1_ssem, r1_rsem, dev(x, py, z, 1)).start()
        loop(1, Y, one)

        def two(i):
            pz = (z + i) % Z
            remote(out_items.at[slab_z(pz)], in_items.at[slab_z(z)], r1_ssem, r1_rsem, dev(x, y, pz, 1)).start()
        loop(1, Z, two)

    def query_part(h):
        return lax.dot_general(grads[h], pool[...], (((0,), (0,)), ((), ())), preferred_element_type=jnp.float32)

    qpart[...] = query_part(1 - c)
    part_copy = remote(qpart, qland, pair_ssem.at[4], pair_rsem.at[4], partner)
    part_copy.start()
    scores[0, pl.ds(0, qd), :] = query_part(c)

    def spread(rows_sum, owners, first):
        n = owners * BLK
        pack[pl.ds(0, n), :] = jnp.zeros((n, 128), jnp.float32)
        for r in range(OWNED):
            for a in range(chunks):
                pack[pl.ds(a * OWNED + r, owners, stride=BLK), :] = \
                    rows_sum[r * owners:(r + 1) * owners, a * 128:(a + 1) * 128]
        pieces[pl.ds(first * BLK, n), :] = pack[pl.ds(0, n), :].astype(jnp.bfloat16)

    @pl.when(c == 0)
    def _():
        bytes_of(in_items.at[pl.ds(0, (X - 1) * slab)], r1_rsem).wait()
        total = out_items[slab0(x), :].astype(jnp.float32)
        for i in range(1, X):
            total = total + in_items[slab0((x + i) % X), :].astype(jnp.float32)
        acc[pl.ds(0, slab), :] = total
        spread(acc[pl.ds(0, slab), :], Y * Z, 0)
        me = y * Z + z
        land2[rows(me), :] = pieces[rows(me), :]

        def one(i):
            py, pz = yz_peer(i)
            remote(pieces.at[rows(py * Z + pz)], land2.at[rows(me)], r2_ssem, r2_rsem, dev(x, py, pz, 0)).start()
        loop(1, Y * Z, one)

    @pl.when(c == 1)
    def _():
        bytes_of(in_items.at[pl.ds(0, (Y - 1) * yrows + (Z - 1) * zrows)], r1_rsem).wait()
        acc[pl.ds(0, yrows), :] = out_items[slab_y(y), :].astype(jnp.float32)
        acc[pl.ds(yrows, zrows), :] = out_items[slab_z(z), :].astype(jnp.float32)

        def one(i):
            acc[pl.ds(0, yrows), :] += in_items[slab_y((y + i) % Y), :].astype(jnp.float32)
        loop(1, Y, one)

        def two(i):
            acc[pl.ds(yrows, zrows), :] += in_items[slab_z((z + i) % Z), :].astype(jnp.float32)
        loop(1, Z, two)
        spread(acc[pl.ds(0, yrows), :], xz_own, 0)
        spread(acc[pl.ds(yrows, zrows), :], xy_own, xz_own)

        def to_even(i):
            px, pz = 2 * (i // Z), i % Z

            @pl.when(jnp.logical_or(px != x, pz != z))
            def _():
                remote(pieces.at[rows(i)], land2.at[rows(x * Z + z)], r2_ssem, r2_rsem, dev(px, y, pz, 1)).start()

            @pl.when(jnp.logical_and(px == x, pz == z))
            def _():
                land2[rows(x * Z + z), :] = pieces[rows(i), :]
        loop(0, xz_own, to_even)

        def to_odd(i):
            px, py = 2 * (i // Y) + 1, i % Y

            @pl.when(jnp.logical_or(px != x, py != y))
            def _():
                remote(pieces.at[rows(xz_own + i)], land2.at[rows(x * Y + y)], r2_ssem, r2_rsem, dev(px, py, z, 1)).start()

            @pl.when(jnp.logical_and(px == x, py == y))
            def _():
                land2[rows(x * Y + y), :] = pieces[rows(xz_own + i), :]
        loop(0, xy_own, to_odd)

    part_copy.wait()
    qg_ref[...] = (scores[0, pl.ds(0, qd), :] + qland[...]).astype(jnp.bfloat16)

    @pl.when(c == 0)
    def _():
        bytes_of(land2.at[pl.ds(0, (Y * Z - 1) * BLK)], r2_rsem).wait()

    @pl.when(c == 1)
    def _():
        bytes_of(land2.at[pl.ds(0, (X * Z - 1) * BLK)], r2_rsem).wait()

    def gather(n):
        def body(i, carry):
            return carry + land2[rows(i), :].astype(jnp.float32)
        pack[pl.ds(0, BLK), :] = lax.fori_loop(0, n, body, jnp.zeros((BLK, 128), jnp.float32))

    @pl.when(c == 0)
    def _():
        gather(Y * Z)

    @pl.when(c == 1)
    def _():
        gather(X * Z)
    for a in range(chunks):
        ig_ref[:, a * 128:(a + 1) * 128] = pack[pl.ds(a * OWNED, OWNED), :]

    @pl.when(c == 0)
    def _():
        bytes_of(land.at[pl.ds(0, (Y * Z - 1) * BLK)], s1_ssem).wait()
        bytes_of(pool.at[pl.ds(0, (X - 1) * slab)], s2_ssem).wait()
        bytes_of(pool.at[pl.ds(0, (X - 1) * slab)], r1_ssem).wait()
        bytes_of(land2.at[pl.ds(0, (Y * Z - 1) * BLK)], r2_ssem).wait()

    @pl.when(c == 1)
    def _():
        bytes_of(land.at[pl.ds(0, (X * Z - 1) * BLK)], s1_ssem).wait()
        bytes_of(pool.at[pl.ds(0, (Y - 1) * yrows + (Z - 1) * zrows)], s2_ssem).wait()
        bytes_of(pool.at[pl.ds(0, (Y - 1) * yrows + (Z - 1) * zrows)], r1_ssem).wait()
        bytes_of(land2.at[pl.ds(0, (X * Z - 1) * BLK)], r2_ssem).wait()


def solution(mesh):
    X = mesh.shape["wide"] // ZHI

    def body(queries, targets, lengths, contrast_items):
        qd, width = queries.shape
        zlo = 4 if mesh.shape["narrow"] == 64 else 1
        Y = mesh.shape["narrow"] // (2 * zlo)
        Z = zlo * ZHI
        items = X * Y * Z * OWNED
        blocks = max(Y * Z, X * Z, X * Y) * BLK
        vmem = pl.BlockSpec(memory_space=pltpu.VMEM)
        f32, bf16 = jnp.float32, jnp.bfloat16
        qg, ig, loss = pl.pallas_call(
            functools.partial(kernel, X, Y, Z),
            out_shape=(
                jax.ShapeDtypeStruct((qd, width), bf16),
                jax.ShapeDtypeStruct((OWNED, width), f32),
                jax.ShapeDtypeStruct((1, qd), f32),
            ),
            in_specs=[pl.BlockSpec(memory_space=pl.ANY), vmem, pl.BlockSpec(memory_space=pltpu.SMEM), vmem],
            out_specs=(vmem, vmem, vmem),
            scratch_shapes=[
                pltpu.VMEM((2, qd, width), bf16),
                pltpu.VMEM((2, 8, qd), f32),
                pltpu.VMEM((2, 2, 8, qd), f32),
                pltpu.VMEM((items, width), bf16),
                pltpu.VMEM((blocks, 128), f32),
                pltpu.VMEM((BLK, 128), bf16),
                pltpu.VMEM((blocks, 128), bf16),
                pltpu.VMEM((2, max(items, qd), qd), f32),
                pltpu.VMEM((2, items, qd), bf16),
                pltpu.VMEM((items, width), bf16),
                pltpu.VMEM((items, width), bf16),
                pltpu.VMEM((items // X, width), f32),
                pltpu.VMEM((blocks, 128), bf16),
                pltpu.VMEM((blocks, 128), bf16),
                pltpu.VMEM((qd, width), f32),
                pltpu.VMEM((qd, width), f32),
                pltpu.SemaphoreType.DMA,
                pltpu.SemaphoreType.DMA((5,)),
                pltpu.SemaphoreType.DMA((5,)),
                *[pltpu.SemaphoreType.DMA] * 8,
            ],
            compiler_params=pltpu.CompilerParams(
                collective_id=0, has_side_effects=True, vmem_limit_bytes=40 << 20),
        )(queries, targets.reshape(1, qd), lengths, contrast_items)
        return qg, ig, loss.reshape(qd)

    rows = P(("wide", "narrow"), None)
    flat = P(("wide", "narrow"))
    return jax.shard_map(
        body, mesh=mesh, in_specs=(rows, flat, flat, rows), out_specs=(rows, rows, flat), check_vma=False)
```

time: 824 us -> 62.1 us (0.08)
  the two profiles are of different devices: /device:TPU:1 before, /device:TPU:8 now
where the time goes in v1:
time: 62.1 us; the launch traced here: 61.9 us
  Pallas kernels  56.2 us (90%)
  local copies, waits for them, and re-layouts  5.03 us (8%)
  between operations  0.65 us (1%)
    pallas_call x1, Pallas kernels, body(): pl.pallas_call(functools.partial(kernel, X, Y, Z), out_shape=(jax.ShapeDt...  56.2 us
    unnamed x11, local copies, waits for them, and re-layouts  5.03 us

profile of v1, /device:TPU:8, one launch (start us, length us, event | category | flops | bytes accessed | tf_op | source)
XLA Modules:
  0.0 61.9 jit_solution(12328175160586296996)
XLA Ops:
  0.6 0.0 copy-start.3
  0.6 0.6 %copy-done.3 = s32[2]{0:T(128)S(1)} copy-done((s32[2]{0:T(128)S(1)}, s32[2]{0:T(128)}, u32[]{:S(2)}) %copy-start.3) | copy-done | bytes 32
  1.3 0.0 copy-start
  1.3 1.0 %copy-done = bf16[512,512]{1,0:T(8,128)(2,1)S(1)} copy-done((bf16[512,512]{1,0:T(8,128)(2,1)S(1)}, bf16[512,512]{1,0:T(8,128)(2,1)}, u32[]{:S(2)}) %copy-start) | copy-done | bytes 524312
  2.3 0.0 copy-start.1
  2.3 0.7 %copy-done.1 = bf16[3,512]{1,0:T(4,128)(2,1)S(1)} copy-done((bf16[3,512]{1,0:T(4,128)(2,1)S(1)}, bf16[3,512]{1,0:T(4,128)(2,1)}, u32[]{:S(2)}) %copy-start.1) | copy-done | bytes 3096
  3.0 0.0 copy-start.2
  3.0 0.7 %copy-done.2 = s32[512]{0:T(512)S(1)} copy-done((s32[512]{0:T(512)S(1)}, s32[512]{0:T(512)}, u32[]{:S(2)}) %copy-start.2) | copy-done | bytes 2072
  3.7 56.2 %shard_map.67 = (bf16[512,512]{1,0:T(8,128)(2,1)S(1)}, f32[3,512]{1,0:T(4,128)S(1)}, f32[1,512]{1,0:T(1,128)S(1)}) custom-call(bf16[512,512]{1,0:T(8,128)(2,1)S(1)} %copy-done, s32[1,512]{1,0:T(1,128)S(1)} %bitcast.2, s32[2]{0:T(128)S(1)} %copy-done.3, bf16[3,512]{1,0:T(4,128)(2,1)S(1)} %copy-done.1), custom_call_target="tpu_custom_call" | custom-call | tf_op jit(solution)/shard_map/pallas_call | solution.py:432
  59.9 0.8 %copy.10 = bf16[512,512]{1,0:T(8,128)(2,1)} copy(bf16[512,512]{1,0:T(8,128)(2,1)S(1)} %get-tuple-element.12) | data formatting | bytes 1048576
  60.7 0.6 copy.11
  61.3 0.6 copy.12
Async XLA Ops:
  0.6 0.7 %copy-start.3 = (s32[2]{0:T(128)S(1)}, s32[2]{0:T(128)}, u32[]{:S(2)}) copy-start(s32[2]{0:T(128)} %len_ref.1) | copy-start | bytes 28
  1.3 1.0 %copy-start = (bf16[512,512]{1,0:T(8,128)(2,1)S(1)}, bf16[512,512]{1,0:T(8,128)(2,1)}, u32[]{:S(2)}) copy-start(bf16[512,512]{1,0:T(8,128)(2,1)} %q_hbm.1) | copy-start | bytes 1572868
  2.3 0.7 %copy-start.1 = (bf16[3,512]{1,0:T(4,128)(2,1)S(1)}, bf16[3,512]{1,0:T(4,128)(2,1)}, u32[]{:S(2)}) copy-start(bf16[3,512]{1,0:T(4,128)(2,1)} %it_ref.1) | copy-start | bytes 9220
  3.0 0.7 %copy-start.2 = (s32[512]{0:T(512)S(1)}, s32[512]{0:T(512)}, u32[]{:S(2)}) copy-start(s32[512]{0:T(512)} %param.5) | copy-start | bytes 6148

commit v2 on v1

--- a/solution.py
+++ b/solution.py
@@ -16,10 +16,23 @@
 BLK = 16
 
 
-def kernel(X, Y, Z, q_hbm, tgt_ref, len_ref, it_ref, qg_ref, ig_ref, loss_ref,
-           q_all, info, stat, pool, pack, blk, land, scores, grads, out_items, in_items,
+def hops(d, n):
+    return min(d % n, -d % n)
+
+
+def far_first(A, B):
+    offsets = [(a, b) for a in range(A) for b in range(B) if a or b]
+    return sorted(offsets, key=lambda o: -hops(o[0], A) - hops(o[1], B))
+
+
+def far_ring(n):
+    return sorted(range(1, n), key=lambda d: -hops(d, n))
+
+
+def kernel(X, Y, Z, q_hbm, tgt_hbm, len_hbm, it_hbm, qg_hbm, ig_hbm, loss_hbm,
+           tgt_ref, len_ref, it_ref, qg_ref, ig_ref, loss_ref, q_all, info, stat, pool, pack, blk, land, scores, grads, out_items, in_items,
            acc, pieces, land2, qpart, qland,
-           q_sem, pair_ssem, pair_rsem, s1_ssem, s1_rsem, s2_ssem, s2_rsem,
+           q_sem, in_sem, out_sem, pair_ssem, pair_rsem, s1_ssem, s1_rsem, s2_ssem, s2_rsem,
            r1_ssem, r1_rsem, r2_ssem, r2_rsem):
     zlo = Z // ZHI
     wide, narrow = lax.axis_index("wide"), lax.axis_index("narrow")
@@ -36,14 +49,7 @@
     def dev(px, py, pz, pc):
         return (px * ZHI + pz // zlo, ((pz % zlo) * Y + py) * 2 + pc)
 
-    def yz_peer(i):
-        return (y + i // Z) % Y, (z + i % Z) % Z
-
-    def xz_peer(i):
-        return (x + i // Z) % X, (z + i % Z) % Z
-
-    def xy_peer(i):
-        return (x + i // Y) % X, (y + i % Y) % Y
+    yz, xz, xy = far_first(Y, Z), far_first(X, Z), far_first(X, Y)
 
     def remote(src, dst, ssem, rsem, to):
         return pltpu.make_async_remote_copy(
@@ -58,7 +64,11 @@
             return carry
         lax.fori_loop(lo, hi, step, 0)
 
+    loads = [pltpu.make_async_copy(a, b, in_sem.at[k])
+             for k, (a, b) in enumerate([(it_hbm, it_ref), (tgt_hbm, tgt_ref), (len_hbm, len_ref)])]
     load_q = pltpu.make_async_copy(q_hbm, q_all.at[c], q_sem)
+    for load in loads:
+        load.start()
     load_q.start()
 
     barrier = pltpu.get_barrier_semaphore()
@@ -67,34 +77,31 @@
     def greet(to):
         pl.semaphore_signal(barrier, inc=1, device_id=to, device_id_type=MESH)
 
+    @pl.when(c == 0)
+    def _():
+        for dy, dz in yz:
+            greet(dev(x, (y + dy) % Y, (z + dz) % Z, 0))
+        for dx in far_ring(X):
+            greet(dev((x + dx) % X, y, z, 0))
+
+    @pl.when(c == 1)
+    def _():
+        for dx, dz in xz:
+            greet(dev((x + dx) % X, y, (z + dz) % Z, 1))
+        for dx, dy in xy:
+            greet(dev((x + dx) % X, (y + dy) % Y, z, 1))
+
     greet(partner)
 
-    @pl.when(c == 0)
-    def _():
-        def one(i):
-            py, pz = yz_peer(i)
-            greet(dev(x, py, pz, 0))
-        loop(1, Y * Z, one)
-        loop(1, X, lambda i: greet(dev((x + i) % X, y, z, 0)))
-
-    @pl.when(c == 1)
-    def _():
-        def one(i):
-            px, pz = xz_peer(i)
-            greet(dev(px, y, pz, 1))
-        loop(1, X * Z, one)
-
-        def two(i):
-            px, py = xy_peer(i)
-            greet(dev(px, py, z, 1))
-        loop(1, X * Y, two)
-
+    loads[0].wait()
     own = it_ref[...].astype(jnp.float32)
     pack[pl.ds(0, BLK), :] = jnp.zeros((BLK, 128), jnp.float32)
     for a in range(chunks):
         pack[pl.ds(a * OWNED, OWNED), :] = own[:, a * 128:(a + 1) * 128]
     blk[...] = pack[pl.ds(0, BLK), :].astype(jnp.bfloat16)
 
+    loads[1].wait()
+    loads[2].wait()
     pos = lax.broadcasted_iota(jnp.int32, (1, qd), 1)
     live = jnp.where(pos < SEQ_LEN, (pos < len_ref[0]).astype(jnp.float32),
                      (pos - SEQ_LEN < len_ref[1]).astype(jnp.float32))
@@ -114,37 +121,29 @@
     def rows(i):
         return pl.ds(pl.multiple_of(i * BLK, BLK), BLK)
 
-    s1_copies = []
-
     @pl.when(c == 0)
     def _():
         me = y * Z + z
         land[rows(me), :] = blk[...]
 
-        def one(i):
-            py, pz = yz_peer(i)
-            remote(blk, land.at[rows(me)], s1_ssem, s1_rsem, dev(x, py, pz, 0)).start()
-        loop(1, Y * Z, one)
+        for dy, dz in yz:
+            remote(blk, land.at[rows(me)], s1_ssem, s1_rsem, dev(x, (y + dy) % Y, (z + dz) % Z, 0)).start()
 
     @pl.when(jnp.logical_and(c == 1, even))
     def _():
         me = (x // 2) * Z + z
         land[rows(me), :] = blk[...]
 
-        def one(i):
-            px, pz = xz_peer(i)
-            remote(blk, land.at[rows(me)], s1_ssem, s1_rsem, dev(px, y, pz, 1)).start()
-        loop(1, X * Z, one)
+        for dx, dz in xz:
+            remote(blk, land.at[rows(me)], s1_ssem, s1_rsem, dev((x + dx) % X, y, (z + dz) % Z, 1)).start()
 
     @pl.when(jnp.logical_and(c == 1, jnp.logical_not(even)))
     def _():
         me = X // 2 * Z + (x // 2) * Y + y
         land[rows(me), :] = blk[...]
 
-        def one(i):
-            px, py = xy_peer(i)
-            remote(blk, land.at[rows(me)], s1_ssem, s1_rsem, dev(px, py, z, 1)).start()
-        loop(1, X * Y, one)
+        for dx, dy in xy:
+            remote(blk, land.at[rows(me)], s1_ssem, s1_rsem, dev((x + dx) % X, (y + dy) % Y, z, 1)).start()
 
     q_copy = remote(q_all.at[c], q_all.at[c], pair_ssem.at[0], pair_rsem.at[0], partner)
     q_copy.start()
@@ -183,24 +182,20 @@
     def _():
         unpack(0, Y * Z, x * slab)
 
-        def one(i):
-            px = (x + i) % X
-            remote(pool.at[slab0(x)], pool.at[slab0(x)], s2_ssem, s2_rsem, dev(px, y, z, 0)).start()
-        loop(1, X, one)
+        for dx in far_ring(X):
+            remote(pool.at[slab0(x)], pool.at[slab0(x)], s2_ssem, s2_rsem, dev((x + dx) % X, y, z, 0)).start()
         bytes_of(pool.at[pl.ds(0, (X - 1) * slab)], s2_rsem).wait()
 
     @pl.when(c == 1)
     def _():
         unpack(0, xz_own, y * yrows)
 
-        def one(i):
-            remote(pool.at[slab_y(y)], pool.at[slab_y(y)], s2_ssem, s2_rsem, dev(x, (y + i) % Y, z, 1)).start()
-        loop(1, Y, one)
+        for dy in far_ring(Y):
+            remote(pool.at[slab_y(y)], pool.at[slab_y(y)], s2_ssem, s2_rsem, dev(x, (y + dy) % Y, z, 1)).start()
         unpack(xz_own, xy_own, half + z * zrows)
 
-        def two(i):
-            remote(pool.at[slab_z(z)], pool.at[slab_z(z)], s2_ssem, s2_rsem, dev(x, y, (z + i) % Z, 1)).start()
-        loop(1, Z, two)
+        for dz in far_ring(Z):
+            remote(pool.at[slab_z(z)], pool.at[slab_z(z)], s2_ssem, s2_rsem, dev(x, y, (z + dz) % Z, 1)).start()
         bytes_of(pool.at[pl.ds(0, (Y - 1) * yrows + (Z - 1) * zrows)], s2_rsem).wait()
 
     q_copy.wait()
@@ -251,7 +246,8 @@
         stat[0, h, pl.ds(3, 5), :] = jnp.zeros((5, qd), jnp.float32)
         remote(stat.at[0, h], stat.at[1, h], pair_ssem.at[2 + h], pair_rsem.at[2 + h], partner).start()
 
-    loop(0, 2, first_pass)
+    first_pass(1 - c)
+    first_pass(c)
 
     def second_pass(h):
         remote(stat.at[0, h], stat.at[1, h], pair_ssem.at[2 + h], pair_rsem.at[2 + h], partner).wait()
@@ -276,39 +272,46 @@
             grads[h, at, :] = g.astype(jnp.bfloat16)
         loop(0, items // step, body)
 
-    loop(0, 2, second_pass)
-
-    def item_tile(i):
-        px = (x + 1 + i) % X
+    def query_part(h):
+        return lax.dot_general(grads[h], pool[...], (((0,), (0,)), ((), ())), preferred_element_type=jnp.float32)
+
+    second_pass(1 - c)
+    qpart[...] = query_part(1 - c)
+    part_copy = remote(qpart, qland, pair_ssem.at[4], pair_rsem.at[4], partner)
+    part_copy.start()
+    second_pass(c)
+
+    per = slab // yrows
+    for dx in far_ring(X) + [0]:
+        px = (x + dx) % X
         at = slab0(px)
         g = jnp.dot(grads[0, at, :], q_all[0], preferred_element_type=jnp.float32)
         g = g + jnp.dot(grads[1, at, :], q_all[1], preferred_element_type=jnp.float32)
         out_items[at, :] = g.astype(jnp.bfloat16)
 
-        @pl.when(jnp.logical_and(c == 0, px != x))
-        def _():
-            remote(out_items.at[at], in_items.at[slab0(x)], r1_ssem, r1_rsem, dev(px, y, z, 0)).start()
-
-    loop(0, X, item_tile)
-
-    @pl.when(c == 1)
-    def _():
-        def one(i):
-            py = (y + i) % Y
-            remote(out_items.at[slab_y(py)], in_items.at[slab_y(y)], r1_ssem, r1_rsem, dev(x, py, z, 1)).start()
-        loop(1, Y, one)
-
-        def two(i):
-            pz = (z + i) % Z
-            remote(out_items.at[slab_z(pz)], in_items.at[slab_z(z)], r1_ssem, r1_rsem, dev(x, y, pz, 1)).start()
-        loop(1, Z, two)
-
-    def query_part(h):
-        return lax.dot_general(grads[h], pool[...], (((0,), (0,)), ((), ())), preferred_element_type=jnp.float32)
-
-    qpart[...] = query_part(1 - c)
-    part_copy = remote(qpart, qland, pair_ssem.at[4], pair_rsem.at[4], partner)
-    part_copy.start()
+        if dx:
+            @pl.when(c == 0)
+            def _():
+                remote(out_items.at[at], in_items.at[slab0(x)], r1_ssem, r1_rsem, dev(px, y, z, 0)).start()
+
+        @pl.when(jnp.logical_and(c == 1, px < X // 2))
+        def _():
+            for j in range(per):
+                py = px * per + j
+
+                @pl.when(py != y)
+                def _():
+                    remote(out_items.at[slab_y(py)], in_items.at[slab_y(y)], r1_ssem, r1_rsem, dev(x, py, z, 1)).start()
+
+        @pl.when(jnp.logical_and(c == 1, px >= X // 2))
+        def _():
+            for j in range(per):
+                pz = (px - X // 2) * per + j
+
+                @pl.when(pz != z)
+                def _():
+                    remote(out_items.at[slab_z(pz)], in_items.at[slab_z(z)], r1_ssem, r1_rsem, dev(x, y, pz, 1)).start()
+
     scores[0, pl.ds(0, qd), :] = query_part(c)
 
     def spread(rows_sum, owners, first):
@@ -331,10 +334,9 @@
         me = y * Z + z
         land2[rows(me), :] = pieces[rows(me), :]
 
-        def one(i):
-            py, pz = yz_peer(i)
+        for dy, dz in yz:
+            py, pz = (y + dy) % Y, (z + dz) % Z
             remote(pieces.at[rows(py * Z + pz)], land2.at[rows(me)], r2_ssem, r2_rsem, dev(x, py, pz, 0)).start()
-        loop(1, Y * Z, one)
 
     @pl.when(c == 1)
     def _():
@@ -352,32 +354,48 @@
         spread(acc[pl.ds(0, yrows), :], xz_own, 0)
         spread(acc[pl.ds(yrows, zrows), :], xy_own, xz_own)
 
-        def to_even(i):
-            px, pz = 2 * (i // Z), i % Z
-
-            @pl.when(jnp.logical_or(px != x, pz != z))
-            def _():
-                remote(pieces.at[rows(i)], land2.at[rows(x * Z + z)], r2_ssem, r2_rsem, dev(px, y, pz, 1)).start()
-
-            @pl.when(jnp.logical_and(px == x, pz == z))
-            def _():
-                land2[rows(x * Z + z), :] = pieces[rows(i), :]
-        loop(0, xz_own, to_even)
-
-        def to_odd(i):
-            px, py = 2 * (i // Y) + 1, i % Y
-
-            @pl.when(jnp.logical_or(px != x, py != y))
-            def _():
-                remote(pieces.at[rows(xz_own + i)], land2.at[rows(x * Y + y)], r2_ssem, r2_rsem, dev(px, py, z, 1)).start()
-
-            @pl.when(jnp.logical_and(px == x, py == y))
-            def _():
-                land2[rows(x * Y + y), :] = pieces[rows(xz_own + i), :]
-        loop(0, xy_own, to_odd)
+        @pl.when(even)
+        def _():
+            land2[rows(x * Z + z), :] = pieces[rows((x // 2) * Z + z), :]
+
+        @pl.when(jnp.logical_not(even))
+        def _():
+            land2[rows(x * Y + y), :] = pieces[rows(xz_own + (x // 2) * Y + y), :]
+
+        def to_xz(dx, dz):
+            px, pz = (x + dx) % X, (z + dz) % Z
+            remote(pieces.at[rows((px // 2) * Z + pz)], land2.at[rows(x * Z + z)],
+                   r2_ssem, r2_rsem, dev(px, y, pz, 1)).start()
+
+        def to_xy(dx, dy):
+            px, py = (x + dx) % X, (y + dy) % Y
+            remote(pieces.at[rows(xz_own + (px // 2) * Y + py)], land2.at[rows(x * Y + y)],
+                   r2_ssem, r2_rsem, dev(px, py, z, 1)).start()
+
+        @pl.when(even)
+        def _():
+            for dx, dz in xz:
+                if dx % 2 == 0:
+                    to_xz(dx, dz)
+            for dx, dy in xy:
+                if dx % 2 == 1:
+                    to_xy(dx, dy)
+
+        @pl.when(jnp.logical_not(even))
+        def _():
+            for dx, dz in xz:
+                if dx % 2 == 1:
+                    to_xz(dx, dz)
+            for dx, dy in xy:
+                if dx % 2 == 0:
+                    to_xy(dx, dy)
 
     part_copy.wait()
     qg_ref[...] = (scores[0, pl.ds(0, qd), :] + qland[...]).astype(jnp.bfloat16)
+    results = [pltpu.make_async_copy(a, b, out_sem.at[k])
+               for k, (a, b) in enumerate([(qg_ref, qg_hbm), (loss_ref, loss_hbm), (ig_ref, ig_hbm)])]
+    results[0].start()
+    results[1].start()
 
     @pl.when(c == 0)
     def _():
@@ -402,6 +420,8 @@
     for a in range(chunks):
         ig_ref[:, a * 128:(a + 1) * 128] = pack[pl.ds(a * OWNED, OWNED), :]
 
+    results[2].start()
+
     @pl.when(c == 0)
     def _():
         bytes_of(land.at[pl.ds(0, (Y * Z - 1) * BLK)], s1_ssem).wait()
@@ -415,6 +435,17 @@
         bytes_of(pool.at[pl.ds(0, (Y - 1) * yrows + (Z - 1) * zrows)], s2_ssem).wait()
         bytes_of(pool.at[pl.ds(0, (Y - 1) * yrows + (Z - 1) * zrows)], r1_ssem).wait()
         bytes_of(land2.at[pl.ds(0, (X * Z - 1) * BLK)], r2_ssem).wait()
+    for result in results:
+        result.wait()
+
+
+def leave(qg, ig, loss, qg_out, ig_out, loss_out, sem):
+    copies = [pltpu.make_async_copy(a, b, sem.at[k])
+              for k, (a, b) in enumerate([(qg, qg_out), (ig, ig_out), (loss, loss_out)])]
+    for copy in copies:
+        copy.start()
+    for copy in copies:
+        copy.wait()
 
 
 def solution(mesh):
@@ -427,18 +458,23 @@
         Z = zlo * ZHI
         items = X * Y * Z * OWNED
         blocks = max(Y * Z, X * Z, X * Y) * BLK
-        vmem = pl.BlockSpec(memory_space=pltpu.VMEM)
+        anywhere = pl.BlockSpec(memory_space=pl.ANY)
         f32, bf16 = jnp.float32, jnp.bfloat16
+        outs = (
+            jax.ShapeDtypeStruct((qd, width), bf16),
+            jax.ShapeDtypeStruct((OWNED, width), f32),
+            jax.ShapeDtypeStruct((1, qd), f32),
+        )
         qg, ig, loss = pl.pallas_call(
             functools.partial(kernel, X, Y, Z),
-            out_shape=(
-                jax.ShapeDtypeStruct((qd, width), bf16),
-                jax.ShapeDtypeStruct((OWNED, width), f32),
-                jax.ShapeDtypeStruct((1, qd), f32),
-            ),
-            in_specs=[pl.BlockSpec(memory_space=pl.ANY), vmem, pl.BlockSpec(memory_space=pltpu.SMEM), vmem],
-            out_specs=(vmem, vmem, vmem),
+            out_shape=outs,
+            in_specs=[anywhere] * 4,
+            out_specs=(anywhere,) * 3,
             scratch_shapes=[
+                pltpu.VMEM((1, qd), jnp.int32),
+                pltpu.SMEM(lengths.shape, jnp.int32),
+                pltpu.VMEM((OWNED, width), bf16),
+                *[pltpu.VMEM(o.shape, o.dtype) for o in outs],
                 pltpu.VMEM((2, qd, width), bf16),
                 pltpu.VMEM((2, 8, qd), f32),
                 pltpu.VMEM((2, 2, 8, qd), f32),
@@ -456,13 +492,20 @@
                 pltpu.VMEM((qd, width), f32),
                 pltpu.VMEM((qd, width), f32),
                 pltpu.SemaphoreType.DMA,
+                pltpu.SemaphoreType.DMA((3,)),
+                pltpu.SemaphoreType.DMA((3,)),
                 pltpu.SemaphoreType.DMA((5,)),
                 pltpu.SemaphoreType.DMA((5,)),
                 *[pltpu.SemaphoreType.DMA] * 8,
             ],
             compiler_params=pltpu.CompilerParams(
-                collective_id=0, has_side_effects=True, vmem_limit_bytes=40 << 20),
+                collective_id=0, has_side_effects=True, vmem_limit_bytes=60 << 20),
         )(queries, targets.reshape(1, qd), lengths, contrast_items)
+        qg, ig, loss = pl.pallas_call(
+            leave, out_shape=outs, in_specs=[anywhere] * 3, out_specs=(anywhere,) * 3,
+            scratch_shapes=[pltpu.SemaphoreType.DMA((3,))],
+            compiler_params=pltpu.CompilerParams(vmem_limit_bytes=60 << 20),
+        )(qg, ig, loss)
         return qg, ig, loss.reshape(qd)
 
     rows = P(("wide", "narrow"), None)

time: 62.1 us -> 70.5 us (1.14)
  the two profiles are of different devices: /device:TPU:8 before, /device:TPU:1 now
where the time goes in v2:
time: 70.5 us; the launch traced here: 70.3 us
  Pallas kernels  69.7 us (99%)
    pallas_call x1, Pallas kernels, body(): pl.pallas_call(functools.partial(kernel, X, Y, Z), out_shape=outs, in_spe...  52.4 us
    pallas_call x1, Pallas kernels, body(): pl.pallas_call(leave, out_shape=outs, in_specs=[anywhere] * 3, out_specs=...  17.3 us

profile of v2, /device:TPU:1, one launch (start us, length us, event | category | flops | bytes accessed | tf_op | source)
XLA Modules:
  0.0 70.3 jit_solution(6814610833997202093)
XLA Ops:
  0.6 52.4 %shard_map.67 = (bf16[512,512]{1,0:T(8,128)(2,1)}, f32[3,512]{1,0:T(4,128)}, f32[1,512]{1,0:T(1,128)}) custom-call(bf16[512,512]{1,0:T(8,128)(2,1)} %q_hbm.1, s32[1,512]{1,0:T(1,128)} %bitcast.2, s32[2]{0:T(128)} %len_hbm.1, bf16[3,512]{1,0:T(4,128)(2,1)} %it_hbm.1), custom_call_target="tpu_custom_call" | custom-call | tf_op jit(solution)/shard_map/pallas_call | solution.py:468
  53.0 17.3 %shard_map.68 = (bf16[512,512]{1,0:T(8,128)(2,1)}, f32[3,512]{1,0:T(4,128)}, f32[1,512]{1,0:T(1,128)}) custom-call(bf16[512,512]{1,0:T(8,128)(2,1)} %get-tuple-element.9.qg, f32[3,512]{1,0:T(4,128)} %get-tuple-element.10.ig, f32[1,512]{1,0:T(1,128)} %get-tuple-element.11.loss), custom_call_target="tpu_custom_call" | custom-call | tf_op jit(solution)/shard_map/pallas_call | solution.py:504

commit v3 on v2

--- a/solution.py
+++ b/solution.py
@@ -439,12 +439,18 @@
         result.wait()
 
 
-def leave(qg, ig, loss, qg_out, ig_out, loss_out, sem):
-    copies = [pltpu.make_async_copy(a, b, sem.at[k])
-              for k, (a, b) in enumerate([(qg, qg_out), (ig, ig_out), (loss, loss_out)])]
-    for copy in copies:
+def leave(qg, ig, loss, qg_out, ig_out, loss_out, qg_v, ig_v, loss_v, in_sem, out_sem):
+    n = qg.shape[0] // 4
+    legs = [(qg.at[pl.ds(i * n, n)], qg_v.at[pl.ds(i * n, n)], qg_out.at[pl.ds(i * n, n)]) for i in range(4)]
+    legs += [(ig, ig_v, ig_out), (loss, loss_v, loss_out)]
+    ins = [pltpu.make_async_copy(a, b, in_sem.at[k]) for k, (a, b, _) in enumerate(legs)]
+    outs = [pltpu.make_async_copy(b, d, out_sem.at[k]) for k, (_, b, d) in enumerate(legs)]
+    for copy in ins:
         copy.start()
-    for copy in copies:
+    for copy, after in zip(ins, outs):
+        copy.wait()
+        after.start()
+    for copy in outs:
         copy.wait()
 
 
@@ -503,7 +509,11 @@
         )(queries, targets.reshape(1, qd), lengths, contrast_items)
         qg, ig, loss = pl.pallas_call(
             leave, out_shape=outs, in_specs=[anywhere] * 3, out_specs=(anywhere,) * 3,
-            scratch_shapes=[pltpu.SemaphoreType.DMA((3,))],
+            scratch_shapes=[
+                *[pltpu.VMEM(o.shape, o.dtype) for o in outs],
+                pltpu.SemaphoreType.DMA((6,)),
+                pltpu.SemaphoreType.DMA((6,)),
+            ],
             compiler_params=pltpu.CompilerParams(vmem_limit_bytes=60 << 20),
         )(qg, ig, loss)
         return qg, ig, loss.reshape(qd)

time: 70.5 us -> 55 us (0.78)
  Pallas kernels: 69.7 us -> 54.2 us
    pallas_call x1, Pallas kernels: 17.3 us -> 1.86 us  [body(): pl.pallas_call(leave, out_shape=outs, in_specs=[anywhere] * 3, out_specs=...]
where the time goes in v3:
time: 55 us; the launch traced here: 54.9 us
  Pallas kernels  54.2 us (99%)
  between operations  0.64 us (1%)
    pallas_call x1, Pallas kernels, body(): pl.pallas_call(functools.partial(kernel, X, Y, Z), out_shape=outs, in_spe...  52.4 us
    pallas_call x1, Pallas kernels, body(): pl.pallas_call(leave, out_shape=outs, in_specs=[anywhere] * 3, out_specs=...  1.86 us

profile of v3, /device:TPU:1, one launch (start us, length us, event | category | flops | bytes accessed | tf_op | source)
XLA Modules:
  0.0 54.9 jit_solution(10674686914785832276)
XLA Ops:
  0.6 52.4 %shard_map.67 = (bf16[512,512]{1,0:T(8,128)(2,1)}, f32[3,512]{1,0:T(4,128)}, f32[1,512]{1,0:T(1,128)}) custom-call(bf16[512,512]{1,0:T(8,128)(2,1)} %q_hbm.1, s32[1,512]{1,0:T(1,128)} %bitcast.2, s32[2]{0:T(128)} %len_hbm.1, bf16[3,512]{1,0:T(4,128)(2,1)} %it_hbm.1), custom_call_target="tpu_custom_call" | custom-call | tf_op jit(solution)/shard_map/pallas_call | solution.py:474
  53.0 1.9 %shard_map.68 = (bf16[512,512]{1,0:T(8,128)(2,1)}, f32[3,512]{1,0:T(4,128)}, f32[1,512]{1,0:T(1,128)}) custom-call(bf16[512,512]{1,0:T(8,128)(2,1)} %get-tuple-element.9.qg, f32[3,512]{1,0:T(4,128)} %get-tuple-element.10.ig, f32[1,512]{1,0:T(1,128)} %get-tuple-element.11.loss), custom_call_target="tpu_custom_call" | custom-call | tf_op jit(solution)/shard_map/pallas_call | solution.py:510

commit v4 on v3

--- a/solution.py
+++ b/solution.py
@@ -29,9 +29,9 @@
     return sorted(range(1, n), key=lambda d: -hops(d, n))
 
 
-def kernel(X, Y, Z, q_hbm, tgt_hbm, len_hbm, it_hbm, qg_hbm, ig_hbm, loss_hbm,
-           tgt_ref, len_ref, it_ref, qg_ref, ig_ref, loss_ref, q_all, info, stat, pool, pack, blk, land, scores, grads, out_items, in_items,
-           acc, pieces, land2, qpart, qland,
+def kernel(X, Y, Z, q_hbm, tgt_hbm, len_hbm, it_hbm, qg_hbm, loss_hbm, land2,
+           tgt_ref, len_ref, it_ref, qg_ref, loss_ref, q_all, info, stat, pool, pack, blk, land, scores, grads, out_items, in_items,
+           acc, pieces, qpart, qland,
            q_sem, in_sem, out_sem, pair_ssem, pair_rsem, s1_ssem, s1_rsem, s2_ssem, s2_rsem,
            r1_ssem, r1_rsem, r2_ssem, r2_rsem):
     zlo = Z // ZHI
@@ -275,43 +275,49 @@
     def query_part(h):
         return lax.dot_general(grads[h], pool[...], (((0,), (0,)), ((), ())), preferred_element_type=jnp.float32)
 
+    per, tiles = slab // yrows, X // 2
+    order0 = [(x + dx) % X for dx in far_ring(X) + [0]]
+    order1 = [p for k in range(1, tiles + 1)
+              for p in ((y // per + k) % tiles, tiles + (z // per + k) % tiles)]
+    order = [jnp.where(c == 0, p, q) for p, q in zip(order0, order1)]
+
     second_pass(1 - c)
+    for px in order:
+        at = slab0(px)
+        scores[1 - c, at, :] = jnp.dot(grads[1 - c, at, :], q_all[1 - c], preferred_element_type=jnp.float32)
+    second_pass(c)
+    for k, px in enumerate(order):
+        at = slab0(px)
+        g = jnp.dot(grads[c, at, :], q_all[c], preferred_element_type=jnp.float32) + scores[1 - c, at, :]
+        out_items[at, :] = g.astype(jnp.bfloat16)
+
+        if k < X - 1:
+            @pl.when(c == 0)
+            def _():
+                remote(out_items.at[at], in_items.at[slab0(x)], r1_ssem, r1_rsem, dev(px, y, z, 0)).start()
+
+        @pl.when(c == 1)
+        def _():
+            for j in range(per):
+                if k % 2 == 0:
+                    py = px * per + j
+
+                    @pl.when(py != y)
+                    def _():
+                        remote(out_items.at[slab_y(py)], in_items.at[slab_y(y)], r1_ssem, r1_rsem, dev(x, py, z, 1)).start()
+                else:
+                    pz = (px - tiles) * per + j
+
+                    @pl.when(pz != z)
+                    def _():
+                        remote(out_items.at[slab_z(pz)], in_items.at[slab_z(z)], r1_ssem, r1_rsem, dev(x, y, pz, 1)).start()
+
+    def query_part(h):
+        return lax.dot_general(grads[h], pool[...], (((0,), (0,)), ((), ())), preferred_element_type=jnp.float32)
+
     qpart[...] = query_part(1 - c)
     part_copy = remote(qpart, qland, pair_ssem.at[4], pair_rsem.at[4], partner)
     part_copy.start()
-    second_pass(c)
-
-    per = slab // yrows
-    for dx in far_ring(X) + [0]:
-        px = (x + dx) % X
-        at = slab0(px)
-        g = jnp.dot(grads[0, at, :], q_all[0], preferred_element_type=jnp.float32)
-        g = g + jnp.dot(grads[1, at, :], q_all[1], preferred_element_type=jnp.float32)
-        out_items[at, :] = g.astype(jnp.bfloat16)
-
-        if dx:
-            @pl.when(c == 0)
-            def _():
-                remote(out_items.at[at], in_items.at[slab0(x)], r1_ssem, r1_rsem, dev(px, y, z, 0)).start()
-
-        @pl.when(jnp.logical_and(c == 1, px < X // 2))
-        def _():
-            for j in range(per):
-                py = px * per + j
-
-                @pl.when(py != y)
-                def _():
-                    remote(out_items.at[slab_y(py)], in_items.at[slab_y(y)], r1_ssem, r1_rsem, dev(x, py, z, 1)).start()
-
-        @pl.when(jnp.logical_and(c == 1, px >= X // 2))
-        def _():
-            for j in range(per):
-                pz = (px - X // 2) * per + j
-
-                @pl.when(pz != z)
-                def _():
-                    remote(out_items.at[slab_z(pz)], in_items.at[slab_z(z)], r1_ssem, r1_rsem, dev(x, y, pz, 1)).start()
-
     scores[0, pl.ds(0, qd), :] = query_part(c)
 
     def spread(rows_sum, owners, first):
@@ -332,7 +338,7 @@
         acc[pl.ds(0, slab), :] = total
         spread(acc[pl.ds(0, slab), :], Y * Z, 0)
         me = y * Z + z
-        land2[rows(me), :] = pieces[rows(me), :]
+        pltpu.make_async_copy(pieces.at[rows(me)], land2.at[rows(me)], out_sem.at[2]).start()
 
         for dy, dz in yz:
             py, pz = (y + dy) % Y, (z + dz) % Z
@@ -356,11 +362,12 @@
 
         @pl.when(even)
         def _():
-            land2[rows(x * Z + z), :] = pieces[rows((x // 2) * Z + z), :]
+            pltpu.make_async_copy(pieces.at[rows((x // 2) * Z + z)], land2.at[rows(x * Z + z)], out_sem.at[2]).start()
 
         @pl.when(jnp.logical_not(even))
         def _():
-            land2[rows(x * Y + y), :] = pieces[rows(xz_own + (x // 2) * Y + y), :]
+            pltpu.make_async_copy(pieces.at[rows(xz_own + (x // 2) * Y + y)], land2.at[rows(x * Y + y)],
+                                  out_sem.at[2]).start()
 
         def to_xz(dx, dz):
             px, pz = (x + dx) % X, (z + dz) % Z
@@ -393,9 +400,9 @@
     part_copy.wait()
     qg_ref[...] = (scores[0, pl.ds(0, qd), :] + qland[...]).astype(jnp.bfloat16)
     results = [pltpu.make_async_copy(a, b, out_sem.at[k])
-               for k, (a, b) in enumerate([(qg_ref, qg_hbm), (loss_ref, loss_hbm), (ig_ref, ig_hbm)])]
-    results[0].start()
-    results[1].start()
+               for k, (a, b) in enumerate([(qg_ref, qg_hbm), (loss_ref, loss_hbm)])]
+    for result in results:
+        result.start()
 
     @pl.when(c == 0)
     def _():
@@ -404,23 +411,6 @@
     @pl.when(c == 1)
     def _():
         bytes_of(land2.at[pl.ds(0, (X * Z - 1) * BLK)], r2_rsem).wait()
-
-    def gather(n):
-        def body(i, carry):
-            return carry + land2[rows(i), :].astype(jnp.float32)
-        pack[pl.ds(0, BLK), :] = lax.fori_loop(0, n, body, jnp.zeros((BLK, 128), jnp.float32))
-
-    @pl.when(c == 0)
-    def _():
-        gather(Y * Z)
-
-    @pl.when(c == 1)
-    def _():
-        gather(X * Z)
-    for a in range(chunks):
-        ig_ref[:, a * 128:(a + 1) * 128] = pack[pl.ds(a * OWNED, OWNED), :]
-
-    results[2].start()
 
     @pl.when(c == 0)
     def _():
@@ -435,23 +425,40 @@
         bytes_of(pool.at[pl.ds(0, (Y - 1) * yrows + (Z - 1) * zrows)], s2_ssem).wait()
         bytes_of(pool.at[pl.ds(0, (Y - 1) * yrows + (Z - 1) * zrows)], r1_ssem).wait()
         bytes_of(land2.at[pl.ds(0, (X * Z - 1) * BLK)], r2_ssem).wait()
+    bytes_of(pieces.at[pl.ds(0, BLK)], out_sem.at[2]).wait()
     for result in results:
         result.wait()
 
 
-def leave(qg, ig, loss, qg_out, ig_out, loss_out, qg_v, ig_v, loss_v, in_sem, out_sem):
+def finish(n0, n1, qg, loss, land2, qg_out, ig_out, loss_out, qg_v, ig_v, loss_v, land_v, total, in_sem, out_sem):
     n = qg.shape[0] // 4
     legs = [(qg.at[pl.ds(i * n, n)], qg_v.at[pl.ds(i * n, n)], qg_out.at[pl.ds(i * n, n)]) for i in range(4)]
-    legs += [(ig, ig_v, ig_out), (loss, loss_v, loss_out)]
+    legs += [(loss, loss_v, loss_out)]
+    land_in = pltpu.make_async_copy(land2, land_v, in_sem.at[5])
+    land_in.start()
     ins = [pltpu.make_async_copy(a, b, in_sem.at[k]) for k, (a, b, _) in enumerate(legs)]
     outs = [pltpu.make_async_copy(b, d, out_sem.at[k]) for k, (_, b, d) in enumerate(legs)]
     for copy in ins:
         copy.start()
+    land_in.wait()
+    group = min(n0, n1, 8)
+
+    def body(i, carry):
+        part = land_v[pl.ds(pl.multiple_of(i * group * BLK, BLK), group * BLK), :].astype(jnp.float32)
+        return carry + jnp.sum(part.reshape(group, BLK, 128), axis=0)
+
+    count = jnp.where(lax.axis_index("narrow") % 2 == 0, n0 // group, n1 // group)
+    total[...] = lax.fori_loop(0, count, body, jnp.zeros((BLK, 128), jnp.float32))
+    for a in range(ig_v.shape[1] // 128):
+        ig_v[:, a * 128:(a + 1) * 128] = total[pl.ds(a * OWNED, OWNED), :]
+    ig_copy = pltpu.make_async_copy(ig_v, ig_out, out_sem.at[5])
+    ig_copy.start()
     for copy, after in zip(ins, outs):
         copy.wait()
         after.start()
     for copy in outs:
         copy.wait()
+    ig_copy.wait()
 
 
 def solution(mesh):
@@ -471,16 +478,17 @@
             jax.ShapeDtypeStruct((OWNED, width), f32),
             jax.ShapeDtypeStruct((1, qd), f32),
         )
-        qg, ig, loss = pl.pallas_call(
+        qg, loss, land2 = pl.pallas_call(
             functools.partial(kernel, X, Y, Z),
-            out_shape=outs,
+            out_shape=(outs[0], outs[2], jax.ShapeDtypeStruct((blocks, 128), bf16)),
             in_specs=[anywhere] * 4,
             out_specs=(anywhere,) * 3,
             scratch_shapes=[
                 pltpu.VMEM((1, qd), jnp.int32),
                 pltpu.SMEM(lengths.shape, jnp.int32),
                 pltpu.VMEM((OWNED, width), bf16),
-                *[pltpu.VMEM(o.shape, o.dtype) for o in outs],
+                pltpu.VMEM((qd, width), bf16),
+                pltpu.VMEM((1, qd), f32),
                 pltpu.VMEM((2, qd, width), bf16),
                 pltpu.VMEM((2, 8, qd), f32),
                 pltpu.VMEM((2, 2, 8, qd), f32),
@@ -493,7 +501,6 @@
                 pltpu.VMEM((items, width), bf16),
                 pltpu.VMEM((items, width), bf16),
                 pltpu.VMEM((items // X, width), f32),
-                pltpu.VMEM((blocks, 128), bf16),
                 pltpu.VMEM((blocks, 128), bf16),
                 pltpu.VMEM((qd, width), f32),
                 pltpu.VMEM((qd, width), f32),
@@ -508,14 +515,16 @@
                 collective_id=0, has_side_effects=True, vmem_limit_bytes=60 << 20),
         )(queries, targets.reshape(1, qd), lengths, contrast_items)
         qg, ig, loss = pl.pallas_call(
-            leave, out_shape=outs, in_specs=[anywhere] * 3, out_specs=(anywhere,) * 3,
+            functools.partial(finish, Y * Z, X * Z), out_shape=outs, in_specs=[anywhere] * 3, out_specs=(anywhere,) * 3,
             scratch_shapes=[
                 *[pltpu.VMEM(o.shape, o.dtype) for o in outs],
+                pltpu.VMEM((blocks, 128), bf16),
+                pltpu.VMEM((BLK, 128), f32),
                 pltpu.SemaphoreType.DMA((6,)),
                 pltpu.SemaphoreType.DMA((6,)),
             ],
             compiler_params=pltpu.CompilerParams(vmem_limit_bytes=60 << 20),
-        )(qg, ig, loss)
+        )(qg, loss, land2)
         return qg, ig, loss.reshape(qd)
 
     rows = P(("wide", "narrow"), None)

time: 55 us -> 53.6 us (0.975); the launches traced: 54.9 us -> 52.7 us
  Pallas kernels: 54.2 us -> 52.1 us
    pallas_call x2, Pallas kernels: 54.2 us -> 52.1 us  [the longest x1 50.2 us: body(): pl.pallas_call(functools.partial(kernel, X, Y, Z), out_shape=(outs[0], ou...]
where the time goes in v4:
time: 53.6 us; the launch traced here: 52.7 us
  Pallas kernels  52.1 us (97%)
  between operations  0.64 us (1%)
    pallas_call x1, Pallas kernels, body(): pl.pallas_call(functools.partial(kernel, X, Y, Z), out_shape=(outs[0], ou...  50.2 us
    pallas_call x1, Pallas kernels, body(): pl.pallas_call(functools.partial(finish, Y * Z, X * Z), out_shape=outs, i...  1.92 us

profile of v4, /device:TPU:1, one launch (start us, length us, event | category | flops | bytes accessed | tf_op | source)
XLA Modules:
  0.0 52.7 jit_solution(113639956588373308)
XLA Ops:
  0.6 50.2 %shard_map.67 = (bf16[512,512]{1,0:T(8,128)(2,1)}, f32[1,512]{1,0:T(1,128)}, bf16[1024,128]{1,0:T(8,128)(2,1)}) custom-call(bf16[512,512]{1,0:T(8,128)(2,1)} %q_hbm.1, s32[1,512]{1,0:T(1,128)} %bitcast.2, s32[2]{0:T(128)} %len_hbm.1, bf16[3,512]{1,0:T(4,128)(2,1)} %it_hbm.1), custom_call_target="tpu_custom_call" | custom-call | tf_op jit(solution)/shard_map/pallas_call | solution.py:481
  50.8 1.9 %shard_map.68 = (bf16[512,512]{1,0:T(8,128)(2,1)}, f32[3,512]{1,0:T(4,128)}, f32[1,512]{1,0:T(1,128)}) custom-call(bf16[512,512]{1,0:T(8,128)(2,1)} %get-tuple-element.9.qg, f32[1,512]{1,0:T(1,128)} %get-tuple-element.10.loss, bf16[1024,128]{1,0:T(8,128)(2,1)} %get-tuple-element.11.land2), custom_call_target="tpu_custom_call" | custom-call | tf_op jit(solution)/shard_map/pallas_call | solution.py:517

commit v5 on v4

--- a/solution.py
+++ b/solution.py
@@ -31,7 +31,7 @@
 
 def kernel(X, Y, Z, q_hbm, tgt_hbm, len_hbm, it_hbm, qg_hbm, loss_hbm, land2,
            tgt_ref, len_ref, it_ref, qg_ref, loss_ref, q_all, info, stat, pool, pack, blk, land, scores, grads, out_items, in_items,
-           acc, pieces, qpart, qland,
+           pieces, qpart, qland,
            q_sem, in_sem, out_sem, pair_ssem, pair_rsem, s1_ssem, s1_rsem, s2_ssem, s2_rsem,
            r1_ssem, r1_rsem, r2_ssem, r2_rsem):
     zlo = Z // ZHI
@@ -44,6 +44,10 @@
     half = X * slab // 2
     yrows, zrows = half // Y, half // Z
     items = X * slab
+    groups, members = Z // 2, 2 * Y
+    grows = members * OWNED
+    tile = X * grows
+    last = Z - 1
     even = x % 2 == 0
 
     def dev(px, py, pz, pc):
@@ -123,19 +127,33 @@
 
     @pl.when(c == 0)
     def _():
-        me = y * Z + z
+        me = z * Y + y
         land[rows(me), :] = blk[...]
 
+        def send(py, pz):
+            remote(blk, land.at[rows(me)], s1_ssem, s1_rsem, dev(x, py, pz, 0)).start()
+
+        for dy in far_ring(Y):
+            send((y + dy) % Y, last)
+        pl.when(z != last)(functools.partial(send, y, last))
         for dy, dz in yz:
-            remote(blk, land.at[rows(me)], s1_ssem, s1_rsem, dev(x, (y + dy) % Y, (z + dz) % Z, 0)).start()
+            pz = (z + dz) % Z
+            pl.when(pz != last)(functools.partial(send, (y + dy) % Y, pz))
 
     @pl.when(jnp.logical_and(c == 1, even))
     def _():
         me = (x // 2) * Z + z
         land[rows(me), :] = blk[...]
 
+        def send(px, pz):
+            remote(blk, land.at[rows(me)], s1_ssem, s1_rsem, dev(px, y, pz, 1)).start()
+
+        for dx in far_ring(X):
+            send((x + dx) % X, last)
+        pl.when(z != last)(functools.partial(send, x, last))
         for dx, dz in xz:
-            remote(blk, land.at[rows(me)], s1_ssem, s1_rsem, dev((x + dx) % X, y, (z + dz) % Z, 1)).start()
+            pz = (z + dz) % Z
+            pl.when(pz != last)(functools.partial(send, (x + dx) % X, pz))
 
     @pl.when(jnp.logical_and(c == 1, jnp.logical_not(even)))
     def _():
@@ -169,33 +187,43 @@
 
     xz_own, xy_own = X // 2 * Z, X // 2 * Y
 
-    def slab0(px):
-        return pl.ds(pl.multiple_of(px * slab, 16), slab)
+    def piece(g, px):
+        return pl.ds(pl.multiple_of(g * tile + px * grows, 16), grows)
+
+    def y_at(py):
+        return half // 2 + py * yrows
+
+    def z_at(pz):
+        return pz * zrows + jnp.where(pz >= Z // 2, half, 0)
 
     def slab_y(py):
-        return pl.ds(pl.multiple_of(py * yrows, 16), yrows)
+        return pl.ds(pl.multiple_of(y_at(py), 16), yrows)
 
     def slab_z(pz):
-        return pl.ds(pl.multiple_of(half + pz * zrows, 16), zrows)
-
-    @pl.when(c == 0)
-    def _():
-        unpack(0, Y * Z, x * slab)
-
-        for dx in far_ring(X):
-            remote(pool.at[slab0(x)], pool.at[slab0(x)], s2_ssem, s2_rsem, dev((x + dx) % X, y, z, 0)).start()
+        return pl.ds(pl.multiple_of(z_at(pz), 16), zrows)
+
+    @pl.when(c == 0)
+    def _():
+        for g in range(groups):
+            unpack(g * members, members, g * tile + x * grows)
+            for dx in far_ring(X):
+                remote(pool.at[piece(g, x)], pool.at[piece(g, x)], s2_ssem, s2_rsem, dev((x + dx) % X, y, z, 0)).start()
         bytes_of(pool.at[pl.ds(0, (X - 1) * slab)], s2_rsem).wait()
 
     @pl.when(c == 1)
     def _():
-        unpack(0, xz_own, y * yrows)
-
+        unpack(xz_own, xy_own, z_at(z))
+
+        def send(pz):
+            remote(pool.at[slab_z(z)], pool.at[slab_z(z)], s2_ssem, s2_rsem, dev(x, y, pz, 1)).start()
+
+        pl.when(z != last)(functools.partial(send, last))
+        for dz in far_ring(Z):
+            pz = (z + dz) % Z
+            pl.when(pz != last)(functools.partial(send, pz))
+        unpack(0, xz_own, y_at(y))
         for dy in far_ring(Y):
             remote(pool.at[slab_y(y)], pool.at[slab_y(y)], s2_ssem, s2_rsem, dev(x, (y + dy) % Y, z, 1)).start()
-        unpack(xz_own, xy_own, half + z * zrows)
-
-        for dz in far_ring(Z):
-            remote(pool.at[slab_z(z)], pool.at[slab_z(z)], s2_ssem, s2_rsem, dev(x, y, (z + dz) % Z, 1)).start()
         bytes_of(pool.at[pl.ds(0, (Y - 1) * yrows + (Z - 1) * zrows)], s2_rsem).wait()
 
     q_copy.wait()
@@ -208,12 +236,12 @@
         w, n = o // (zlo * Y * 2), o % (zlo * Y * 2)
         tx, tc = w // ZHI, n % 2
         ty, tz = (n // 2) % Y, (w % ZHI) * zlo + n // (2 * Y)
-        on0 = tx * slab + r * (Y * Z) + ty * Z + tz
-        on1 = jnp.where(tx % 2 == 0, ty * yrows + r * xz_own + (tx // 2) * Z + tz,
-                        half + tz * zrows + r * xy_own + (tx // 2) * Y + ty)
+        on0 = (tz // 2) * tile + tx * grows + r * members + (tz % 2) * Y + ty
+        on1 = jnp.where(tx % 2 == 0, y_at(ty) + r * xz_own + (tx // 2) * Z + tz,
+                        z_at(tz) + r * xy_own + (tx // 2) * Y + ty)
         return jnp.where(tc == c, jnp.where(tc == 0, on0, on1), -1)
 
-    tile = items // 3
+    third = items // 3
     step = max(8, items // 12)
     fold = functools.partial(jnp.reshape, shape=(step // 8, 8, qd))
     row_iota = lax.broadcasted_iota(jnp.int32, (step, qd), 0)
@@ -222,10 +250,10 @@
     def first_pass(h):
         m8 = jnp.full((8, qd), -3e38, jnp.float32)
         for i in range(3):
-            s = lax.dot_general(pool[pl.ds(i * tile, tile), :], q_all[h], (((1,), (1,)), ((), ())),
+            s = lax.dot_general(pool[pl.ds(i * third, third), :], q_all[h], (((1,), (1,)), ((), ())),
                                 preferred_element_type=jnp.float32)
-            scores[h, pl.ds(i * tile, tile), :] = s
-            m8 = jnp.maximum(m8, jnp.max(s.reshape(tile // 8, 8, qd), axis=0))
+            scores[h, pl.ds(i * third, third), :] = s
+            m8 = jnp.maximum(m8, jnp.max(s.reshape(third // 8, 8, qd), axis=0))
         m = jnp.max(m8, axis=0, keepdims=True)
         target = local_row(h)
 
@@ -272,45 +300,39 @@
             grads[h, at, :] = g.astype(jnp.bfloat16)
         loop(0, items // step, body)
 
-    def query_part(h):
-        return lax.dot_general(grads[h], pool[...], (((0,), (0,)), ((), ())), preferred_element_type=jnp.float32)
-
-    per, tiles = slab // yrows, X // 2
-    order0 = [(x + dx) % X for dx in far_ring(X) + [0]]
-    order1 = [p for k in range(1, tiles + 1)
-              for p in ((y // per + k) % tiles, tiles + (z // per + k) % tiles)]
-    order = [jnp.where(c == 0, p, q) for p, q in zip(order0, order1)]
-
     second_pass(1 - c)
-    for px in order:
-        at = slab0(px)
+    for g in range(groups):
+        at = pl.ds(g * tile, tile)
         scores[1 - c, at, :] = jnp.dot(grads[1 - c, at, :], q_all[1 - c], preferred_element_type=jnp.float32)
     second_pass(c)
-    for k, px in enumerate(order):
-        at = slab0(px)
-        g = jnp.dot(grads[c, at, :], q_all[c], preferred_element_type=jnp.float32) + scores[1 - c, at, :]
-        out_items[at, :] = g.astype(jnp.bfloat16)
-
-        if k < X - 1:
-            @pl.when(c == 0)
-            def _():
-                remote(out_items.at[at], in_items.at[slab0(x)], r1_ssem, r1_rsem, dev(px, y, z, 0)).start()
+
+    slabs = [(0, i) for i in range(Z // 2)] + [(1, i) for i in range(Y)] + [(0, i) for i in range(Z // 2, Z)]
+    per = len(slabs) // groups
+    for g in range(groups):
+        at = pl.ds(g * tile, tile)
+        total = jnp.dot(grads[c, at, :], q_all[c], preferred_element_type=jnp.float32) + scores[1 - c, at, :]
+        out_items[at, :] = total.astype(jnp.bfloat16)
+
+        @pl.when(c == 0)
+        def _():
+            for dx in far_ring(X):
+                px = (x + dx) % X
+                remote(out_items.at[piece(g, px)], in_items.at[piece(g, x)],
+                       r1_ssem, r1_rsem.at[g], dev(px, y, z, 0)).start()
 
         @pl.when(c == 1)
         def _():
-            for j in range(per):
-                if k % 2 == 0:
-                    py = px * per + j
-
-                    @pl.when(py != y)
+            for kind, i in slabs[g * per:(g + 1) * per]:
+                if kind == 0:
+                    @pl.when(z != i)
                     def _():
-                        remote(out_items.at[slab_y(py)], in_items.at[slab_y(y)], r1_ssem, r1_rsem, dev(x, py, z, 1)).start()
+                        remote(out_items.at[slab_z(i)], in_items.at[slab_z(z)],
+                               r1_ssem, r1_rsem.at[0], dev(x, y, i, 1)).start()
                 else:
-                    pz = (px - tiles) * per + j
-
-                    @pl.when(pz != z)
+                    @pl.when(y != i)
                     def _():
-                        remote(out_items.at[slab_z(pz)], in_items.at[slab_z(z)], r1_ssem, r1_rsem, dev(x, y, pz, 1)).start()
+                        remote(out_items.at[slab_y(i)], in_items.at[slab_y(y)],
+                               r1_ssem, r1_rsem.at[1], dev(x, i, z, 1)).start()
 
     def query_part(h):
         return lax.dot_general(grads[h], pool[...], (((0,), (0,)), ((), ())), preferred_element_type=jnp.float32)
@@ -329,73 +351,62 @@
                     rows_sum[r * owners:(r + 1) * owners, a * 128:(a + 1) * 128]
         pieces[pl.ds(first * BLK, n), :] = pack[pl.ds(0, n), :].astype(jnp.bfloat16)
 
-    @pl.when(c == 0)
-    def _():
-        bytes_of(in_items.at[pl.ds(0, (X - 1) * slab)], r1_rsem).wait()
-        total = out_items[slab0(x), :].astype(jnp.float32)
-        for i in range(1, X):
-            total = total + in_items[slab0((x + i) % X), :].astype(jnp.float32)
-        acc[pl.ds(0, slab), :] = total
-        spread(acc[pl.ds(0, slab), :], Y * Z, 0)
-        me = y * Z + z
-        pltpu.make_async_copy(pieces.at[rows(me)], land2.at[rows(me)], out_sem.at[2]).start()
-
-        for dy, dz in yz:
-            py, pz = (y + dy) % Y, (z + dz) % Z
-            remote(pieces.at[rows(py * Z + pz)], land2.at[rows(me)], r2_ssem, r2_rsem, dev(x, py, pz, 0)).start()
-
-    @pl.when(c == 1)
-    def _():
-        bytes_of(in_items.at[pl.ds(0, (Y - 1) * yrows + (Z - 1) * zrows)], r1_rsem).wait()
-        acc[pl.ds(0, yrows), :] = out_items[slab_y(y), :].astype(jnp.float32)
-        acc[pl.ds(yrows, zrows), :] = out_items[slab_z(z), :].astype(jnp.float32)
-
-        def one(i):
-            acc[pl.ds(0, yrows), :] += in_items[slab_y((y + i) % Y), :].astype(jnp.float32)
-        loop(1, Y, one)
-
-        def two(i):
-            acc[pl.ds(yrows, zrows), :] += in_items[slab_z((z + i) % Z), :].astype(jnp.float32)
-        loop(1, Z, two)
-        spread(acc[pl.ds(0, yrows), :], xz_own, 0)
-        spread(acc[pl.ds(yrows, zrows), :], xy_own, xz_own)
-
-        @pl.when(even)
-        def _():
-            pltpu.make_async_copy(pieces.at[rows((x // 2) * Z + z)], land2.at[rows(x * Z + z)], out_sem.at[2]).start()
-
-        @pl.when(jnp.logical_not(even))
-        def _():
-            pltpu.make_async_copy(pieces.at[rows(xz_own + (x // 2) * Y + y)], land2.at[rows(x * Y + y)],
-                                  out_sem.at[2]).start()
-
-        def to_xz(dx, dz):
-            px, pz = (x + dx) % X, (z + dz) % Z
-            remote(pieces.at[rows((px // 2) * Z + pz)], land2.at[rows(x * Z + z)],
-                   r2_ssem, r2_rsem, dev(px, y, pz, 1)).start()
-
-        def to_xy(dx, dy):
-            px, py = (x + dx) % X, (y + dy) % Y
-            remote(pieces.at[rows(xz_own + (px // 2) * Y + py)], land2.at[rows(x * Y + y)],
-                   r2_ssem, r2_rsem, dev(px, py, z, 1)).start()
-
-        @pl.when(even)
-        def _():
-            for dx, dz in xz:
-                if dx % 2 == 0:
-                    to_xz(dx, dz)
-            for dx, dy in xy:
-                if dx % 2 == 1:
-                    to_xy(dx, dy)
-
-        @pl.when(jnp.logical_not(even))
-        def _():
-            for dx, dz in xz:
-                if dx % 2 == 1:
-                    to_xz(dx, dz)
-            for dx, dy in xy:
-                if dx % 2 == 0:
-                    to_xy(dx, dy)
+    def keep(block, slot):
+        pltpu.make_async_copy(pieces.at[rows(block)], land2.at[rows(slot)], out_sem.at[2]).start()
+
+    def deliver(block, slot, to):
+        remote(pieces.at[rows(block)], land2.at[rows(slot)], r2_ssem, r2_rsem, to).start()
+
+    @pl.when(c == 0)
+    def _():
+        me = z * Y + y
+        for g in range(groups):
+            bytes_of(in_items.at[pl.ds(0, (X - 1) * grows)], r1_rsem.at[g]).wait()
+            total = out_items[piece(g, x), :].astype(jnp.float32)
+            for i in range(1, X):
+                total = total + in_items[piece(g, (x + i) % X), :].astype(jnp.float32)
+            spread(total, members, g * members)
+            for pz in (2 * g, 2 * g + 1):
+                for dy in far_ring(Y):
+                    py = (y + dy) % Y
+                    deliver(pz * Y + py, me, dev(x, py, pz, 0))
+                pl.when(z != pz)(functools.partial(deliver, pz * Y + y, me, dev(x, y, pz, 0)))
+            pl.when(z // 2 == g)(functools.partial(keep, me, me))
+
+    @pl.when(c == 1)
+    def _():
+        def of_kind(k):
+            @pl.when(k == 0)
+            def _():
+                bytes_of(in_items.at[pl.ds(0, (Z - 1) * zrows)], r1_rsem.at[0]).wait()
+                total = out_items[slab_z(z), :].astype(jnp.float32)
+                for i in range(1, Z):
+                    total = total + in_items[slab_z((z + i) % Z), :].astype(jnp.float32)
+                spread(total, xy_own, xz_own)
+                me = x * Y + y
+                for py in range(Y):
+                    for px in range(1, X, 2):
+                        block = xz_own + (px // 2) * Y + py
+                        here = jnp.logical_and(px == x, py == y)
+                        pl.when(jnp.logical_not(here))(functools.partial(deliver, block, me, dev(px, py, z, 1)))
+                        pl.when(here)(functools.partial(keep, block, me))
+
+            @pl.when(k == 1)
+            def _():
+                bytes_of(in_items.at[pl.ds(0, (Y - 1) * yrows)], r1_rsem.at[1]).wait()
+                total = out_items[slab_y(y), :].astype(jnp.float32)
+                for i in range(1, Y):
+                    total = total + in_items[slab_y((y + i) % Y), :].astype(jnp.float32)
+                spread(total, xz_own, 0)
+                me = x * Z + z
+                for pz in range(Z):
+                    for px in range(0, X, 2):
+                        block = (px // 2) * Z + pz
+                        here = jnp.logical_and(px == x, pz == z)
+                        pl.when(jnp.logical_not(here))(functools.partial(deliver, block, me, dev(px, y, pz, 1)))
+                        pl.when(here)(functools.partial(keep, block, me))
+
+        loop(0, 2, lambda i: of_kind(jnp.where(z < Z // 2, i, 1 - i)))
 
     part_copy.wait()
     qg_ref[...] = (scores[0, pl.ds(0, qd), :] + qland[...]).astype(jnp.bfloat16)
@@ -500,7 +511,6 @@
                 pltpu.VMEM((2, items, qd), bf16),
                 pltpu.VMEM((items, width), bf16),
                 pltpu.VMEM((items, width), bf16),
-                pltpu.VMEM((items // X, width), f32),
                 pltpu.VMEM((blocks, 128), bf16),
                 pltpu.VMEM((qd, width), f32),
                 pltpu.VMEM((qd, width), f32),
@@ -509,7 +519,9 @@
                 pltpu.SemaphoreType.DMA((3,)),
                 pltpu.SemaphoreType.DMA((5,)),
                 pltpu.SemaphoreType.DMA((5,)),
-                *[pltpu.SemaphoreType.DMA] * 8,
+                *[pltpu.SemaphoreType.DMA] * 5,
+                pltpu.SemaphoreType.DMA((max(Z // 2, 2),)),
+                *[pltpu.SemaphoreType.DMA] * 2,
             ],
             compiler_params=pltpu.CompilerParams(
                 collective_id=0, has_side_effects=True, vmem_limit_bytes=60 << 20),

time: 53.6 us -> 52.7 us (0.983)
  the two profiles are of different devices: /device:TPU:1 before, /device:TPU:17 now
where the time goes in v5:
time: 52.7 us; the launch traced here: 52.6 us
  Pallas kernels  51.9 us (98%)
  between operations  0.64 us (1%)
    pallas_call x1, Pallas kernels, body(): pl.pallas_call(functools.partial(kernel, X, Y, Z), out_shape=(outs[0], ou...  50 us
    pallas_call x1, Pallas kernels, body(): pl.pallas_call(functools.partial(finish, Y * Z, X * Z), out_shape=outs, i...  1.92 us

profile of v5, /device:TPU:17, one launch (start us, length us, event | category | flops | bytes accessed | tf_op | source)
XLA Modules:
  0.0 52.6 jit_solution(1790061866950756532)
XLA Ops:
  0.6 50.0 %shard_map.67 = (bf16[512,512]{1,0:T(8,128)(2,1)}, f32[1,512]{1,0:T(1,128)}, bf16[1024,128]{1,0:T(8,128)(2,1)}) custom-call(bf16[512,512]{1,0:T(8,128)(2,1)} %q_hbm.1, s32[1,512]{1,0:T(1,128)} %bitcast.2, s32[2]{0:T(128)} %len_hbm.1, bf16[3,512]{1,0:T(4,128)(2,1)} %it_hbm.1), custom_call_target="tpu_custom_call" | custom-call | tf_op jit(solution)/shard_map/pallas_call | solution.py:492
  50.7 1.9 %shard_map.68 = (bf16[512,512]{1,0:T(8,128)(2,1)}, f32[3,512]{1,0:T(4,128)}, f32[1,512]{1,0:T(1,128)}) custom-call(bf16[512,512]{1,0:T(8,128)(2,1)} %get-tuple-element.9.qg, f32[1,512]{1,0:T(1,128)} %get-tuple-element.10.loss, bf16[1024,128]{1,0:T(8,128)(2,1)} %get-tuple-element.11.land2), custom_call_target="tpu_custom_call" | custom-call | tf_op jit(solution)/shard_map/pallas_call | solution.py:529

commit v6 on v5

--- a/solution.py
+++ b/solution.py
@@ -48,6 +48,7 @@
     grows = members * OWNED
     tile = X * grows
     last = Z - 1
+    near = sorted(range(groups), key=lambda k: hops(k, groups))
     even = x % 2 == 0
 
     def dev(px, py, pz, pc):
@@ -131,7 +132,7 @@
         land[rows(me), :] = blk[...]
 
         def send(py, pz):
-            remote(blk, land.at[rows(me)], s1_ssem, s1_rsem, dev(x, py, pz, 0)).start()
+            remote(blk, land.at[rows(me)], s1_ssem, s1_rsem.at[z // 2], dev(x, py, pz, 0)).start()
 
         for dy in far_ring(Y):
             send((y + dy) % Y, last)
@@ -146,7 +147,7 @@
         land[rows(me), :] = blk[...]
 
         def send(px, pz):
-            remote(blk, land.at[rows(me)], s1_ssem, s1_rsem, dev(px, y, pz, 1)).start()
+            remote(blk, land.at[rows(me)], s1_ssem, s1_rsem.at[1], dev(px, y, pz, 1)).start()
 
         for dx in far_ring(X):
             send((x + dx) % X, last)
@@ -161,24 +162,19 @@
         land[rows(me), :] = blk[...]
 
         for dx, dy in xy:
-            remote(blk, land.at[rows(me)], s1_ssem, s1_rsem, dev((x + dx) % X, (y + dy) % Y, z, 1)).start()
+            remote(blk, land.at[rows(me)], s1_ssem, s1_rsem.at[0], dev((x + dx) % X, (y + dy) % Y, z, 1)).start()
 
     q_copy = remote(q_all.at[c], q_all.at[c], pair_ssem.at[0], pair_rsem.at[0], partner)
     q_copy.start()
     info_copy = remote(info.at[c], info.at[c], pair_ssem.at[1], pair_rsem.at[1], partner)
     info_copy.start()
 
-    @pl.when(c == 0)
-    def _():
-        bytes_of(land.at[pl.ds(0, (Y * Z - 1) * BLK)], s1_rsem).wait()
-
-    @pl.when(c == 1)
-    def _():
-        bytes_of(land.at[pl.ds(0, (X * Z - 1) * BLK)], s1_rsem).wait()
+    def landed(count, k):
+        bytes_of(land.at[pl.ds(0, count * BLK)], s1_rsem.at[k]).wait()
 
     def unpack(first, owners, base):
         n = owners * BLK
-        pack[pl.ds(0, n), :] = land[pl.ds(first * BLK, n), :].astype(jnp.float32)
+        pack[pl.ds(0, n), :] = land[pl.ds(pl.multiple_of(first * BLK, BLK), n), :].astype(jnp.float32)
         for r in range(OWNED):
             for a in range(chunks):
                 piece = pack[pl.ds(a * OWNED + r, owners, stride=BLK), :]
@@ -204,27 +200,34 @@
 
     @pl.when(c == 0)
     def _():
-        for g in range(groups):
+        for k in near:
+            g = (z // 2 + k) % groups
+            landed(members - (k == 0), g)
             unpack(g * members, members, g * tile + x * grows)
             for dx in far_ring(X):
-                remote(pool.at[piece(g, x)], pool.at[piece(g, x)], s2_ssem, s2_rsem, dev((x + dx) % X, y, z, 0)).start()
-        bytes_of(pool.at[pl.ds(0, (X - 1) * slab)], s2_rsem).wait()
+                remote(pool.at[piece(g, x)], pool.at[piece(g, x)],
+                       s2_ssem, s2_rsem.at[g], dev((x + dx) % X, y, z, 0)).start()
 
     @pl.when(c == 1)
     def _():
+        pl.when(even)(functools.partial(landed, xy_own, 0))
+        pl.when(jnp.logical_not(even))(functools.partial(landed, xy_own - 1, 0))
         unpack(xz_own, xy_own, z_at(z))
 
         def send(pz):
-            remote(pool.at[slab_z(z)], pool.at[slab_z(z)], s2_ssem, s2_rsem, dev(x, y, pz, 1)).start()
+            remote(pool.at[slab_z(z)], pool.at[slab_z(z)], s2_ssem, s2_rsem.at[0], dev(x, y, pz, 1)).start()
 
         pl.when(z != last)(functools.partial(send, last))
         for dz in far_ring(Z):
             pz = (z + dz) % Z
             pl.when(pz != last)(functools.partial(send, pz))
+
+        pl.when(even)(functools.partial(landed, xz_own - 1, 1))
+        pl.when(jnp.logical_not(even))(functools.partial(landed, xz_own, 1))
         unpack(0, xz_own, y_at(y))
         for dy in far_ring(Y):
-            remote(pool.at[slab_y(y)], pool.at[slab_y(y)], s2_ssem, s2_rsem, dev(x, (y + dy) % Y, z, 1)).start()
-        bytes_of(pool.at[pl.ds(0, (Y - 1) * yrows + (Z - 1) * zrows)], s2_rsem).wait()
+            remote(pool.at[slab_y(y)], pool.at[slab_y(y)],
+                   s2_ssem, s2_rsem.at[1], dev(x, (y + dy) % Y, z, 1)).start()
 
     q_copy.wait()
     info_copy.wait()
@@ -241,19 +244,34 @@
                         z_at(tz) + r * xy_own + (tx // 2) * Y + ty)
         return jnp.where(tc == c, jnp.where(tc == 0, on0, on1), -1)
 
-    third = items // 3
     step = max(8, items // 12)
     fold = functools.partial(jnp.reshape, shape=(step // 8, 8, qd))
     row_iota = lax.broadcasted_iota(jnp.int32, (step, qd), 0)
     K = SHARPNESS * LOG2E
 
-    def first_pass(h):
-        m8 = jnp.full((8, qd), -3e38, jnp.float32)
-        for i in range(3):
-            s = lax.dot_general(pool[pl.ds(i * third, third), :], q_all[h], (((1,), (1,)), ((), ())),
-                                preferred_element_type=jnp.float32)
-            scores[h, pl.ds(i * third, third), :] = s
-            m8 = jnp.maximum(m8, jnp.max(s.reshape(third // 8, 8, qd), axis=0))
+    halves = (1 - c, c)
+    tops = [jnp.full((8, qd), -3e38, jnp.float32)] * 2
+    for k in range(groups):
+        g = jnp.where(c == 0, (z // 2 + near[k]) % groups, k)
+
+        @pl.when(c == 0)
+        def _():
+            bytes_of(pool.at[pl.ds(0, (X - 1) * grows)], s2_rsem.at[g]).wait()
+
+        @pl.when(c == 1)
+        def _():
+            if k == 0:
+                bytes_of(pool.at[pl.ds(0, (Z - 1) * zrows)], s2_rsem.at[0]).wait()
+            if k == min(1, groups - 1):
+                bytes_of(pool.at[pl.ds(0, (Y - 1) * yrows)], s2_rsem.at[1]).wait()
+
+        at = pl.ds(pl.multiple_of(g * tile, 16), tile)
+        for i, h in enumerate(halves):
+            s = lax.dot_general(pool[at, :], q_all[h], (((1,), (1,)), ((), ())), preferred_element_type=jnp.float32)
+            scores[h, at, :] = s
+            tops[i] = jnp.maximum(tops[i], jnp.max(s.reshape(tile // 8, 8, qd), axis=0))
+
+    def first_pass(h, m8):
         m = jnp.max(m8, axis=0, keepdims=True)
         target = local_row(h)
 
@@ -274,8 +292,8 @@
         stat[0, h, pl.ds(3, 5), :] = jnp.zeros((5, qd), jnp.float32)
         remote(stat.at[0, h], stat.at[1, h], pair_ssem.at[2 + h], pair_rsem.at[2 + h], partner).start()
 
-    first_pass(1 - c)
-    first_pass(c)
+    for h, m8 in zip(halves, tops):
+        first_pass(h, m8)
 
     def second_pass(h):
         remote(stat.at[0, h], stat.at[1, h], pair_ssem.at[2 + h], pair_rsem.at[2 + h], partner).wait()
@@ -519,8 +537,7 @@
                 pltpu.SemaphoreType.DMA((3,)),
                 pltpu.SemaphoreType.DMA((5,)),
                 pltpu.SemaphoreType.DMA((5,)),
-                *[pltpu.SemaphoreType.DMA] * 5,
-                pltpu.SemaphoreType.DMA((max(Z // 2, 2),)),
+                *[pltpu.SemaphoreType.DMA, pltpu.SemaphoreType.DMA((max(Z // 2, 2),))] * 3,
                 *[pltpu.SemaphoreType.DMA] * 2,
             ],
             compiler_params=pltpu.CompilerParams(

time: 52.7 us -> 49.4 us (0.937)
  the two profiles are of different devices: /device:TPU:17 before, /device:TPU:1 now
where the time goes in v6:
time: 49.4 us; the launch traced here: 49.1 us
  Pallas kernels  48.5 us (98%)
  between operations  0.64 us (1%)
    pallas_call x1, Pallas kernels, body(): pl.pallas_call(functools.partial(kernel, X, Y, Z), out_shape=(outs[0], ou...  46.6 us
    pallas_call x1, Pallas kernels, body(): pl.pallas_call(functools.partial(finish, Y * Z, X * Z), out_shape=outs, i...  1.92 us

profile of v6, /device:TPU:1, one launch (start us, length us, event | category | flops | bytes accessed | tf_op | source)
XLA Modules:
  0.0 49.1 jit_solution(6129047139166905385)
XLA Ops:
  0.6 46.6 %shard_map.67 = (bf16[512,512]{1,0:T(8,128)(2,1)}, f32[1,512]{1,0:T(1,128)}, bf16[1024,128]{1,0:T(8,128)(2,1)}) custom-call(bf16[512,512]{1,0:T(8,128)(2,1)} %q_hbm.1, s32[1,512]{1,0:T(1,128)} %bitcast.2, s32[2]{0:T(128)} %len_hbm.1, bf16[3,512]{1,0:T(4,128)(2,1)} %it_hbm.1), custom_call_target="tpu_custom_call" | custom-call | tf_op jit(solution)/shard_map/pallas_call | solution.py:510
  47.2 1.9 %shard_map.68 = (bf16[512,512]{1,0:T(8,128)(2,1)}, f32[3,512]{1,0:T(4,128)}, f32[1,512]{1,0:T(1,128)}) custom-call(bf16[512,512]{1,0:T(8,128)(2,1)} %get-tuple-element.9.qg, f32[1,512]{1,0:T(1,128)} %get-tuple-element.10.loss, bf16[1024,128]{1,0:T(8,128)(2,1)} %get-tuple-element.11.land2), custom_call_target="tpu_custom_call" | custom-call | tf_op jit(solution)/shard_map/pallas_call | solution.py:546

commit v7 on v6

--- a/solution.py
+++ b/solution.py
@@ -30,7 +30,7 @@
 
 
 def kernel(X, Y, Z, q_hbm, tgt_hbm, len_hbm, it_hbm, qg_hbm, loss_hbm, land2,
-           tgt_ref, len_ref, it_ref, qg_ref, loss_ref, q_all, info, stat, pool, pack, blk, land, scores, grads, out_items, in_items,
+           tgt_ref, len_ref, it_ref, qg_ref, loss_ref, q_all, info, stat, pool, pack, blk, land, scores, tops, grads, out_items, in_items,
            pieces, qpart, qland,
            q_sem, in_sem, out_sem, pair_ssem, pair_rsem, s1_ssem, s1_rsem, s2_ssem, s2_rsem,
            r1_ssem, r1_rsem, r2_ssem, r2_rsem):
@@ -187,10 +187,10 @@
         return pl.ds(pl.multiple_of(g * tile + px * grows, 16), grows)
 
     def y_at(py):
-        return half // 2 + py * yrows
+        return py * yrows
 
     def z_at(pz):
-        return pz * zrows + jnp.where(pz >= Z // 2, half, 0)
+        return half + pz * zrows
 
     def slab_y(py):
         return pl.ds(pl.multiple_of(y_at(py), 16), yrows)
@@ -250,9 +250,11 @@
     K = SHARPNESS * LOG2E
 
     halves = (1 - c, c)
-    tops = [jnp.full((8, qd), -3e38, jnp.float32)] * 2
+    targets = [local_row(h) for h in halves]
+    zero = jnp.zeros((8, qd), jnp.float32)
+    found = [zero, zero]
     for k in range(groups):
-        g = jnp.where(c == 0, (z // 2 + near[k]) % groups, k)
+        g = jnp.where(c == 0, (z // 2 + near[k]) % groups, (groups // 2 + k) % groups)
 
         @pl.when(c == 0)
         def _():
@@ -262,69 +264,75 @@
         def _():
             if k == 0:
                 bytes_of(pool.at[pl.ds(0, (Z - 1) * zrows)], s2_rsem.at[0]).wait()
-            if k == min(1, groups - 1):
+            if k == groups // 2:
                 bytes_of(pool.at[pl.ds(0, (Y - 1) * yrows)], s2_rsem.at[1]).wait()
 
         at = pl.ds(pl.multiple_of(g * tile, 16), tile)
         for i, h in enumerate(halves):
             s = lax.dot_general(pool[at, :], q_all[h], (((1,), (1,)), ((), ())), preferred_element_type=jnp.float32)
             scores[h, at, :] = s
-            tops[i] = jnp.maximum(tops[i], jnp.max(s.reshape(tile // 8, 8, qd), axis=0))
-
-    def first_pass(h, m8):
-        m = jnp.max(m8, axis=0, keepdims=True)
-        target = local_row(h)
-
-        def body(i, carry):
-            l8, t8 = carry
-            at = pl.ds(pl.multiple_of(i * step, 8), step)
-            s = scores[h, at, :]
-            hit = row_iota == target - i * step
-            e = jnp.exp2((s - m) * K)
-            scores[h, at, :] = e
-            return l8 + jnp.sum(fold(e), axis=0), t8 + jnp.sum(fold(jnp.where(hit, s, 0.0)), axis=0)
-
-        zero = jnp.zeros((8, qd), jnp.float32)
-        l8, t8 = lax.fori_loop(0, items // step, body, (zero, zero))
+            m = jnp.max(jnp.max(s.reshape(tile // 8, 8, qd), axis=0), axis=0, keepdims=True)
+
+            def body(j, carry, g=g, h=h, m=m, target=targets[i]):
+                l8, t8 = carry
+                first = pl.multiple_of(g * tile + j * step, 8)
+                at = pl.ds(first, step)
+                s = scores[h, at, :]
+                e = jnp.exp2((s - m) * K)
+                scores[h, at, :] = e
+                hit = row_iota == target - first
+                return l8 + jnp.sum(fold(e), axis=0), t8 + jnp.sum(fold(jnp.where(hit, s, 0.0)), axis=0)
+
+            l8, found[i] = lax.fori_loop(0, tile // step, body, (zero, found[i]))
+            tops[g, h, pl.ds(0, 1), :] = m
+            tops[g, h, pl.ds(1, 1), :] = jnp.sum(l8, axis=0, keepdims=True)
+
+    for i, h in enumerate(halves):
+        m = tops[0, h, pl.ds(0, 1), :]
+        for g in range(1, groups):
+            m = jnp.maximum(m, tops[g, h, pl.ds(0, 1), :])
+        l = jnp.zeros((1, qd), jnp.float32)
+        for g in range(groups):
+            l = l + tops[g, h, pl.ds(1, 1), :] * jnp.exp2((tops[g, h, pl.ds(0, 1), :] - m) * K)
         stat[0, h, pl.ds(0, 1), :] = m
-        stat[0, h, pl.ds(1, 1), :] = jnp.sum(l8, axis=0, keepdims=True)
-        stat[0, h, pl.ds(2, 1), :] = jnp.sum(t8, axis=0, keepdims=True)
+        stat[0, h, pl.ds(1, 1), :] = l
+        stat[0, h, pl.ds(2, 1), :] = jnp.sum(found[i], axis=0, keepdims=True)
         stat[0, h, pl.ds(3, 5), :] = jnp.zeros((5, qd), jnp.float32)
         remote(stat.at[0, h], stat.at[1, h], pair_ssem.at[2 + h], pair_rsem.at[2 + h], partner).start()
 
-    for h, m8 in zip(halves, tops):
-        first_pass(h, m8)
-
-    def second_pass(h):
+    def second_pass(h, target):
         remote(stat.at[0, h], stat.at[1, h], pair_ssem.at[2 + h], pair_rsem.at[2 + h], partner).wait()
         m, l, t = (stat[0, h, pl.ds(k, 1), :] for k in range(3))
         m2, l2, t2 = (stat[1, h, pl.ds(k, 1), :] for k in range(3))
         top = jnp.maximum(m, m2)
-        mine = jnp.exp2((m - top) * K)
-        total = l * mine + l2 * jnp.exp2((m2 - top) * K)
+        total = l * jnp.exp2((m - top) * K) + l2 * jnp.exp2((m2 - top) * K)
         valid = info[h, pl.ds(1, 1), :]
         weight = SHARPNESS * valid
-        factor = weight * mine / total
-        target = local_row(h)
+        share = weight / total
 
         @pl.when(h == c)
         def _():
             loss_ref[...] = valid * (SHARPNESS * (top - (t + t2)) + jnp.log(total))
 
-        def body(i):
-            at = pl.ds(pl.multiple_of(i * step, 16), step)
-            hit = row_iota == target - i * step
-            g = scores[h, at, :] * factor - jnp.where(hit, weight, 0.0)
-            grads[h, at, :] = g.astype(jnp.bfloat16)
-        loop(0, items // step, body)
-
-    second_pass(1 - c)
+        def of_tile(g):
+            factor = share * jnp.exp2((tops[g, h, pl.ds(0, 1), :] - top) * K)
+
+            def body(j):
+                first = pl.multiple_of(g * tile + j * step, 16)
+                at = pl.ds(first, step)
+                hit = row_iota == target - first
+                grad = scores[h, at, :] * factor - jnp.where(hit, weight, 0.0)
+                grads[h, at, :] = grad.astype(jnp.bfloat16)
+            loop(0, tile // step, body)
+        loop(0, groups, of_tile)
+
+    second_pass(1 - c, targets[0])
     for g in range(groups):
         at = pl.ds(g * tile, tile)
         scores[1 - c, at, :] = jnp.dot(grads[1 - c, at, :], q_all[1 - c], preferred_element_type=jnp.float32)
-    second_pass(c)
-
-    slabs = [(0, i) for i in range(Z // 2)] + [(1, i) for i in range(Y)] + [(0, i) for i in range(Z // 2, Z)]
+    second_pass(c, targets[1])
+
+    slabs = [(1, i) for i in range(Y)] + [(0, i) for i in range(Z)]
     per = len(slabs) // groups
     for g in range(groups):
         at = pl.ds(g * tile, tile)
@@ -393,38 +401,21 @@
 
     @pl.when(c == 1)
     def _():
-        def of_kind(k):
-            @pl.when(k == 0)
-            def _():
-                bytes_of(in_items.at[pl.ds(0, (Z - 1) * zrows)], r1_rsem.at[0]).wait()
-                total = out_items[slab_z(z), :].astype(jnp.float32)
-                for i in range(1, Z):
-                    total = total + in_items[slab_z((z + i) % Z), :].astype(jnp.float32)
-                spread(total, xy_own, xz_own)
-                me = x * Y + y
-                for py in range(Y):
-                    for px in range(1, X, 2):
-                        block = xz_own + (px // 2) * Y + py
-                        here = jnp.logical_and(px == x, py == y)
-                        pl.when(jnp.logical_not(here))(functools.partial(deliver, block, me, dev(px, py, z, 1)))
-                        pl.when(here)(functools.partial(keep, block, me))
-
-            @pl.when(k == 1)
-            def _():
-                bytes_of(in_items.at[pl.ds(0, (Y - 1) * yrows)], r1_rsem.at[1]).wait()
-                total = out_items[slab_y(y), :].astype(jnp.float32)
-                for i in range(1, Y):
-                    total = total + in_items[slab_y((y + i) % Y), :].astype(jnp.float32)
-                spread(total, xz_own, 0)
-                me = x * Z + z
-                for pz in range(Z):
-                    for px in range(0, X, 2):
-                        block = (px // 2) * Z + pz
-                        here = jnp.logical_and(px == x, pz == z)
-                        pl.when(jnp.logical_not(here))(functools.partial(deliver, block, me, dev(px, y, pz, 1)))
-                        pl.when(here)(functools.partial(keep, block, me))
-
-        loop(0, 2, lambda i: of_kind(jnp.where(z < Z // 2, i, 1 - i)))
+        def deliver_all(rows_of, n, me, k, first, dests):
+            bytes_of(in_items.at[pl.ds(0, (n - 1) * yrows)], r1_rsem.at[k]).wait()
+            total = out_items[rows_of(me), :].astype(jnp.float32)
+            for i in range(1, n):
+                total = total + in_items[rows_of((me + i) % n), :].astype(jnp.float32)
+            spread(total, len(dests), first)
+            for i, (px, py, pz, slot) in enumerate(dests):
+                here = jnp.logical_and(px == x, jnp.logical_and(py == y, pz == z))
+                pl.when(jnp.logical_not(here))(functools.partial(deliver, first + i, slot, dev(px, py, pz, 1)))
+                pl.when(here)(functools.partial(keep, first + i, slot))
+
+        deliver_all(slab_y, Y, y, 1, 0,
+                    [(px, y, pz, x * Z + z) for px in range(0, X, 2) for pz in range(Z)])
+        deliver_all(slab_z, Z, z, 0, xz_own,
+                    [(px, py, z, x * Y + y) for px in range(1, X, 2) for py in range(Y)])
 
     part_copy.wait()
     qg_ref[...] = (scores[0, pl.ds(0, qd), :] + qland[...]).astype(jnp.bfloat16)
@@ -526,6 +517,7 @@
                 pltpu.VMEM((BLK, 128), bf16),
                 pltpu.VMEM((blocks, 128), bf16),
                 pltpu.VMEM((2, max(items, qd), qd), f32),
+                pltpu.VMEM((Z // 2, 2, 8, qd), f32),
                 pltpu.VMEM((2, items, qd), bf16),
                 pltpu.VMEM((items, width), bf16),
                 pltpu.VMEM((items, width), bf16),

time: 49.4 us -> 49.8 us (level)
  no operation moved by 1% of the time
where the time goes in v7:
time: 49.8 us; the launch traced here: 49.4 us
  Pallas kernels  48.8 us (98%)
  between operations  0.64 us (1%)
    pallas_call x1, Pallas kernels, body(): pl.pallas_call(functools.partial(kernel, X, Y, Z), out_shape=(outs[0], ou...  46.9 us
    pallas_call x1, Pallas kernels, body(): pl.pallas_call(functools.partial(finish, Y * Z, X * Z), out_shape=outs, i...  1.92 us

profile of v7, /device:TPU:1, one launch (start us, length us, event | category | flops | bytes accessed | tf_op | source)
XLA Modules:
  0.0 49.4 jit_solution(9790781068001005500)
XLA Ops:
  0.6 46.9 %shard_map.67 = (bf16[512,512]{1,0:T(8,128)(2,1)}, f32[1,512]{1,0:T(1,128)}, bf16[1024,128]{1,0:T(8,128)(2,1)}) custom-call(bf16[512,512]{1,0:T(8,128)(2,1)} %q_hbm.1, s32[1,512]{1,0:T(1,128)} %bitcast.2, s32[2]{0:T(128)} %len_hbm.1, bf16[3,512]{1,0:T(4,128)(2,1)} %it_hbm.1), custom_call_target="tpu_custom_call" | custom-call | tf_op jit(solution)/shard_map/pallas_call | solution.py:501
  47.5 1.9 %shard_map.68 = (bf16[512,512]{1,0:T(8,128)(2,1)}, f32[3,512]{1,0:T(4,128)}, f32[1,512]{1,0:T(1,128)}) custom-call(bf16[512,512]{1,0:T(8,128)(2,1)} %get-tuple-element.9.qg, f32[1,512]{1,0:T(1,128)} %get-tuple-element.10.loss, bf16[1024,128]{1,0:T(8,128)(2,1)} %get-tuple-element.11.land2), custom_call_target="tpu_custom_call" | custom-call | tf_op jit(solution)/shard_map/pallas_call | solution.py:538

commit v8 on v7

--- a/solution.py
+++ b/solution.py
@@ -72,9 +72,7 @@
     loads = [pltpu.make_async_copy(a, b, in_sem.at[k])
              for k, (a, b) in enumerate([(it_hbm, it_ref), (tgt_hbm, tgt_ref), (len_hbm, len_ref)])]
     load_q = pltpu.make_async_copy(q_hbm, q_all.at[c], q_sem)
-    for load in loads:
-        load.start()
-    load_q.start()
+    loads[0].start()
 
     barrier = pltpu.get_barrier_semaphore()
     partner = dev(x, y, z, 1 - c)
@@ -97,6 +95,9 @@
             greet(dev((x + dx) % X, (y + dy) % Y, z, 1))
 
     greet(partner)
+    loads[1].start()
+    loads[2].start()
+    load_q.start()
 
     loads[0].wait()
     own = it_ref[...].astype(jnp.float32)
@@ -104,6 +105,55 @@
     for a in range(chunks):
         pack[pl.ds(a * OWNED, OWNED), :] = own[:, a * 128:(a + 1) * 128]
     blk[...] = pack[pl.ds(0, BLK), :].astype(jnp.bfloat16)
+
+    @pl.when(c == 0)
+    def _():
+        pl.semaphore_wait(barrier, Y * Z - 1 + X - 1 + 1)
+
+    @pl.when(c == 1)
+    def _():
+        pl.semaphore_wait(barrier, X * Z - 1 + X * Y - 1 + 1)
+
+    def rows(i):
+        return pl.ds(pl.multiple_of(i * BLK, BLK), BLK)
+
+    @pl.when(c == 0)
+    def _():
+        me = z * Y + y
+        land[rows(me), :] = blk[...]
+
+        def send(py, pz):
+            remote(blk, land.at[rows(me)], s1_ssem, s1_rsem.at[z // 2], dev(x, py, pz, 0)).start()
+
+        for dy in far_ring(Y):
+            send((y + dy) % Y, last)
+        pl.when(z != last)(functools.partial(send, y, last))
+        for dy, dz in yz:
+            pz = (z + dz) % Z
+            pl.when(pz != last)(functools.partial(send, (y + dy) % Y, pz))
+
+    @pl.when(jnp.logical_and(c == 1, even))
+    def _():
+        me = (x // 2) * Z + z
+        land[rows(me), :] = blk[...]
+
+        def send(px, pz):
+            remote(blk, land.at[rows(me)], s1_ssem, s1_rsem.at[1], dev(px, y, pz, 1)).start()
+
+        for dx in far_ring(X):
+            send((x + dx) % X, last)
+        pl.when(z != last)(functools.partial(send, x, last))
+        for dx, dz in xz:
+            pz = (z + dz) % Z
+            pl.when(pz != last)(functools.partial(send, (x + dx) % X, pz))
+
+    @pl.when(jnp.logical_and(c == 1, jnp.logical_not(even)))
+    def _():
+        me = X // 2 * Z + (x // 2) * Y + y
+        land[rows(me), :] = blk[...]
+
+        for dx, dy in xy:
+            remote(blk, land.at[rows(me)], s1_ssem, s1_rsem.at[0], dev((x + dx) % X, (y + dy) % Y, z, 1)).start()
 
     loads[1].wait()
     loads[2].wait()
@@ -114,55 +164,6 @@
     info[c, pl.ds(1, 1), :] = live
     info[c, pl.ds(2, 6), :] = jnp.zeros((6, qd), jnp.float32)
     load_q.wait()
-
-    @pl.when(c == 0)
-    def _():
-        pl.semaphore_wait(barrier, Y * Z - 1 + X - 1 + 1)
-
-    @pl.when(c == 1)
-    def _():
-        pl.semaphore_wait(barrier, X * Z - 1 + X * Y - 1 + 1)
-
-    def rows(i):
-        return pl.ds(pl.multiple_of(i * BLK, BLK), BLK)
-
-    @pl.when(c == 0)
-    def _():
-        me = z * Y + y
-        land[rows(me), :] = blk[...]
-
-        def send(py, pz):
-            remote(blk, land.at[rows(me)], s1_ssem, s1_rsem.at[z // 2], dev(x, py, pz, 0)).start()
-
-        for dy in far_ring(Y):
-            send((y + dy) % Y, last)
-        pl.when(z != last)(functools.partial(send, y, last))
-        for dy, dz in yz:
-            pz = (z + dz) % Z
-            pl.when(pz != last)(functools.partial(send, (y + dy) % Y, pz))
-
-    @pl.when(jnp.logical_and(c == 1, even))
-    def _():
-        me = (x // 2) * Z + z
-        land[rows(me), :] = blk[...]
-
-        def send(px, pz):
-            remote(blk, land.at[rows(me)], s1_ssem, s1_rsem.at[1], dev(px, y, pz, 1)).start()
-
-        for dx in far_ring(X):
-            send((x + dx) % X, last)
-        pl.when(z != last)(functools.partial(send, x, last))
-        for dx, dz in xz:
-            pz = (z + dz) % Z
-            pl.when(pz != last)(functools.partial(send, (x + dx) % X, pz))
-
-    @pl.when(jnp.logical_and(c == 1, jnp.logical_not(even)))
-    def _():
-        me = X // 2 * Z + (x // 2) * Y + y
-        land[rows(me), :] = blk[...]
-
-        for dx, dy in xy:
-            remote(blk, land.at[rows(me)], s1_ssem, s1_rsem.at[0], dev((x + dx) % X, (y + dy) % Y, z, 1)).start()
 
     q_copy = remote(q_all.at[c], q_all.at[c], pair_ssem.at[0], pair_rsem.at[0], partner)
     q_copy.start()
@@ -253,6 +254,19 @@
     targets = [local_row(h) for h in halves]
     zero = jnp.zeros((8, qd), jnp.float32)
     found = [zero, zero]
+    def join(h, t8):
+        m = tops[0, h, pl.ds(0, 1), :]
+        for g in range(1, groups):
+            m = jnp.maximum(m, tops[g, h, pl.ds(0, 1), :])
+        l = jnp.zeros((1, qd), jnp.float32)
+        for g in range(groups):
+            l = l + tops[g, h, pl.ds(1, 1), :] * jnp.exp2((tops[g, h, pl.ds(0, 1), :] - m) * K)
+        stat[0, h, pl.ds(0, 1), :] = m
+        stat[0, h, pl.ds(1, 1), :] = l
+        stat[0, h, pl.ds(2, 1), :] = jnp.sum(t8, axis=0, keepdims=True)
+        stat[0, h, pl.ds(3, 5), :] = jnp.zeros((5, qd), jnp.float32)
+        remote(stat.at[0, h], stat.at[1, h], pair_ssem.at[2 + h], pair_rsem.at[2 + h], partner).start()
+
     for k in range(groups):
         g = jnp.where(c == 0, (z // 2 + near[k]) % groups, (groups // 2 + k) % groups)
 
@@ -286,57 +300,41 @@
             l8, found[i] = lax.fori_loop(0, tile // step, body, (zero, found[i]))
             tops[g, h, pl.ds(0, 1), :] = m
             tops[g, h, pl.ds(1, 1), :] = jnp.sum(l8, axis=0, keepdims=True)
-
-    for i, h in enumerate(halves):
-        m = tops[0, h, pl.ds(0, 1), :]
-        for g in range(1, groups):
-            m = jnp.maximum(m, tops[g, h, pl.ds(0, 1), :])
-        l = jnp.zeros((1, qd), jnp.float32)
-        for g in range(groups):
-            l = l + tops[g, h, pl.ds(1, 1), :] * jnp.exp2((tops[g, h, pl.ds(0, 1), :] - m) * K)
-        stat[0, h, pl.ds(0, 1), :] = m
-        stat[0, h, pl.ds(1, 1), :] = l
-        stat[0, h, pl.ds(2, 1), :] = jnp.sum(found[i], axis=0, keepdims=True)
-        stat[0, h, pl.ds(3, 5), :] = jnp.zeros((5, qd), jnp.float32)
-        remote(stat.at[0, h], stat.at[1, h], pair_ssem.at[2 + h], pair_rsem.at[2 + h], partner).start()
-
-    def second_pass(h, target):
+            if k == groups - 1:
+                join(h, found[i])
+
+    def shares(h):
         remote(stat.at[0, h], stat.at[1, h], pair_ssem.at[2 + h], pair_rsem.at[2 + h], partner).wait()
         m, l, t = (stat[0, h, pl.ds(k, 1), :] for k in range(3))
         m2, l2, t2 = (stat[1, h, pl.ds(k, 1), :] for k in range(3))
         top = jnp.maximum(m, m2)
         total = l * jnp.exp2((m - top) * K) + l2 * jnp.exp2((m2 - top) * K)
         valid = info[h, pl.ds(1, 1), :]
-        weight = SHARPNESS * valid
-        share = weight / total
-
-        @pl.when(h == c)
-        def _():
-            loss_ref[...] = valid * (SHARPNESS * (top - (t + t2)) + jnp.log(total))
-
-        def of_tile(g):
-            factor = share * jnp.exp2((tops[g, h, pl.ds(0, 1), :] - top) * K)
-
-            def body(j):
-                first = pl.multiple_of(g * tile + j * step, 16)
-                at = pl.ds(first, step)
-                hit = row_iota == target - first
-                grad = scores[h, at, :] * factor - jnp.where(hit, weight, 0.0)
-                grads[h, at, :] = grad.astype(jnp.bfloat16)
-            loop(0, tile // step, body)
-        loop(0, groups, of_tile)
-
-    second_pass(1 - c, targets[0])
-    for g in range(groups):
-        at = pl.ds(g * tile, tile)
-        scores[1 - c, at, :] = jnp.dot(grads[1 - c, at, :], q_all[1 - c], preferred_element_type=jnp.float32)
-    second_pass(c, targets[1])
+        return top, total, valid, t + t2
+
+    sums = [shares(h) for h in halves]
+
+    def gradients(g, i):
+        top, total, valid, _ = sums[i]
+        h, target, weight = halves[i], targets[i], SHARPNESS * valid
+        factor = weight / total * jnp.exp2((tops[g, h, pl.ds(0, 1), :] - top) * K)
+
+        def body(j):
+            first = pl.multiple_of(g * tile + j * step, 16)
+            at = pl.ds(first, step)
+            hit = row_iota == target - first
+            grad = scores[h, at, :] * factor - jnp.where(hit, weight, 0.0)
+            grads[h, at, :] = grad.astype(jnp.bfloat16)
+        loop(0, tile // step, body)
 
     slabs = [(1, i) for i in range(Y)] + [(0, i) for i in range(Z)]
     per = len(slabs) // groups
     for g in range(groups):
         at = pl.ds(g * tile, tile)
-        total = jnp.dot(grads[c, at, :], q_all[c], preferred_element_type=jnp.float32) + scores[1 - c, at, :]
+        for i in range(2):
+            gradients(g, i)
+        total = jnp.dot(grads[0, at, :], q_all[0], preferred_element_type=jnp.float32)
+        total = total + jnp.dot(grads[1, at, :], q_all[1], preferred_element_type=jnp.float32)
         out_items[at, :] = total.astype(jnp.bfloat16)
 
         @pl.when(c == 0)
@@ -360,6 +358,9 @@
                         remote(out_items.at[slab_y(i)], in_items.at[slab_y(y)],
                                r1_ssem, r1_rsem.at[1], dev(x, i, z, 1)).start()
 
+    top, total, valid, found_score = sums[1]
+    loss_ref[...] = valid * (SHARPNESS * (top - found_score) + jnp.log(total))
+
     def query_part(h):
         return lax.dot_general(grads[h], pool[...], (((0,), (0,)), ((), ())), preferred_element_type=jnp.float32)
 
@@ -454,20 +455,28 @@
     n = qg.shape[0] // 4
     legs = [(qg.at[pl.ds(i * n, n)], qg_v.at[pl.ds(i * n, n)], qg_out.at[pl.ds(i * n, n)]) for i in range(4)]
     legs += [(loss, loss_v, loss_out)]
-    land_in = pltpu.make_async_copy(land2, land_v, in_sem.at[5])
-    land_in.start()
+    core = lax.axis_index("narrow") % 2
+    counts = (n0, n1)
+
+    def land_in(k):
+        part = pl.ds(0, counts[k] * BLK)
+        return pltpu.make_async_copy(land2.at[part], land_v.at[part], in_sem.at[5])
+
+    for k in range(2):
+        pl.when(core == k)(land_in(k).start)
     ins = [pltpu.make_async_copy(a, b, in_sem.at[k]) for k, (a, b, _) in enumerate(legs)]
     outs = [pltpu.make_async_copy(b, d, out_sem.at[k]) for k, (_, b, d) in enumerate(legs)]
     for copy in ins:
         copy.start()
-    land_in.wait()
+    for k in range(2):
+        pl.when(core == k)(land_in(k).wait)
     group = min(n0, n1, 8)
 
     def body(i, carry):
         part = land_v[pl.ds(pl.multiple_of(i * group * BLK, BLK), group * BLK), :].astype(jnp.float32)
         return carry + jnp.sum(part.reshape(group, BLK, 128), axis=0)
 
-    count = jnp.where(lax.axis_index("narrow") % 2 == 0, n0 // group, n1 // group)
+    count = jnp.where(core == 0, n0 // group, n1 // group)
     total[...] = lax.fori_loop(0, count, body, jnp.zeros((BLK, 128), jnp.float32))
     for a in range(ig_v.shape[1] // 128):
         ig_v[:, a * 128:(a + 1) * 128] = total[pl.ds(a * OWNED, OWNED), :]

time: 49.8 us -> 48.7 us (0.978)
  Pallas kernels: 48.8 us -> 47.7 us
    pallas_call x1, Pallas kernels: 46.9 us -> 45.8 us  [body(): pl.pallas_call(functools.partial(kernel, X, Y, Z), out_shape=(outs[0], ou...]
where the time goes in v8:
time: 48.7 us; the launch traced here: 48.4 us
  Pallas kernels  47.7 us (98%)
  between operations  0.64 us (1%)
    pallas_call x1, Pallas kernels, body(): pl.pallas_call(functools.partial(kernel, X, Y, Z), out_shape=(outs[0], ou...  45.8 us
    pallas_call x1, Pallas kernels, body(): pl.pallas_call(functools.partial(finish, Y * Z, X * Z), out_shape=outs, i...  1.94 us

profile of v8, /device:TPU:1, one launch (start us, length us, event | category | flops | bytes accessed | tf_op | source)
XLA Modules:
  0.0 48.4 jit_solution(2851677927009481253)
XLA Ops:
  0.6 45.8 %shard_map.67 = (bf16[512,512]{1,0:T(8,128)(2,1)}, f32[1,512]{1,0:T(1,128)}, bf16[1024,128]{1,0:T(8,128)(2,1)}) custom-call(bf16[512,512]{1,0:T(8,128)(2,1)} %q_hbm.1, s32[1,512]{1,0:T(1,128)} %bitcast.2, s32[2]{0:T(128)} %len_hbm.1, bf16[3,512]{1,0:T(4,128)(2,1)} %it_hbm.1), custom_call_target="tpu_custom_call" | custom-call | tf_op jit(solution)/shard_map/pallas_call | solution.py:510
  46.4 1.9 %shard_map.68 = (bf16[512,512]{1,0:T(8,128)(2,1)}, f32[3,512]{1,0:T(4,128)}, f32[1,512]{1,0:T(1,128)}) custom-call(bf16[512,512]{1,0:T(8,128)(2,1)} %get-tuple-element.9.qg, f32[1,512]{1,0:T(1,128)} %get-tuple-element.10.loss, bf16[1024,128]{1,0:T(8,128)(2,1)} %get-tuple-element.11.land2), custom_call_target="tpu_custom_call" | custom-call | tf_op jit(solution)/shard_map/pallas_call | solution.py:547

commit v9 on v8

--- a/solution.py
+++ b/solution.py
@@ -297,7 +297,9 @@
                 hit = row_iota == target - first
                 return l8 + jnp.sum(fold(e), axis=0), t8 + jnp.sum(fold(jnp.where(hit, s, 0.0)), axis=0)
 
-            l8, found[i] = lax.fori_loop(0, tile // step, body, (zero, found[i]))
+            l8 = zero
+            for j in range(tile // step):
+                l8, found[i] = body(j, (l8, found[i]))
             tops[g, h, pl.ds(0, 1), :] = m
             tops[g, h, pl.ds(1, 1), :] = jnp.sum(l8, axis=0, keepdims=True)
             if k == groups - 1:
@@ -325,7 +327,8 @@
             hit = row_iota == target - first
             grad = scores[h, at, :] * factor - jnp.where(hit, weight, 0.0)
             grads[h, at, :] = grad.astype(jnp.bfloat16)
-        loop(0, tile // step, body)
+        for j in range(tile // step):
+            body(j)
 
     slabs = [(1, i) for i in range(Y)] + [(0, i) for i in range(Z)]
     per = len(slabs) // groups
@@ -408,15 +411,15 @@
             for i in range(1, n):
                 total = total + in_items[rows_of((me + i) % n), :].astype(jnp.float32)
             spread(total, len(dests), first)
-            for i, (px, py, pz, slot) in enumerate(dests):
+            for i, px, py, pz, slot in dests:
                 here = jnp.logical_and(px == x, jnp.logical_and(py == y, pz == z))
                 pl.when(jnp.logical_not(here))(functools.partial(deliver, first + i, slot, dev(px, py, pz, 1)))
                 pl.when(here)(functools.partial(keep, first + i, slot))
 
         deliver_all(slab_y, Y, y, 1, 0,
-                    [(px, y, pz, x * Z + z) for px in range(0, X, 2) for pz in range(Z)])
+                    [(px // 2 * Z + pz, px, y, pz, x * Z + z) for pz in range(Z) for px in range(0, X, 2)])
         deliver_all(slab_z, Z, z, 0, xz_own,
-                    [(px, py, z, x * Y + y) for px in range(1, X, 2) for py in range(Y)])
+                    [(px // 2 * Y + py, px, py, z, x * Y + y) for py in range(Y) for px in range(1, X, 2)])
 
     part_copy.wait()
     qg_ref[...] = (scores[0, pl.ds(0, qd), :] + qland[...]).astype(jnp.bfloat16)

time: 48.7 us -> 48.3 us (level); the launches traced: 48.4 us -> 47.4 us
  Pallas kernels: 47.7 us -> 46.8 us
    pallas_call x1, Pallas kernels: 45.8 us -> 44.9 us  [body(): pl.pallas_call(functools.partial(kernel, X, Y, Z), out_shape=(outs[0], ou...]
where the time goes in v9:
time: 48.3 us; the launch traced here: 47.4 us
  Pallas kernels  46.8 us (97%)
  between operations  0.64 us (1%)
    pallas_call x1, Pallas kernels, body(): pl.pallas_call(functools.partial(kernel, X, Y, Z), out_shape=(outs[0], ou...  44.9 us
    pallas_call x1, Pallas kernels, body(): pl.pallas_call(functools.partial(finish, Y * Z, X * Z), out_shape=outs, i...  1.94 us

profile of v9, /device:TPU:1, one launch (start us, length us, event | category | flops | bytes accessed | tf_op | source)
XLA Modules:
  0.0 47.4 jit_solution(4123305012216095190)
XLA Ops:
  0.6 44.9 %shard_map.67 = (bf16[512,512]{1,0:T(8,128)(2,1)}, f32[1,512]{1,0:T(1,128)}, bf16[1024,128]{1,0:T(8,128)(2,1)}) custom-call(bf16[512,512]{1,0:T(8,128)(2,1)} %q_hbm.1, s32[1,512]{1,0:T(1,128)} %bitcast.2, s32[2]{0:T(128)} %len_hbm.1, bf16[3,512]{1,0:T(4,128)(2,1)} %it_hbm.1), custom_call_target="tpu_custom_call" | custom-call | tf_op jit(solution)/shard_map/pallas_call | solution.py:513
  45.5 1.9 %shard_map.68 = (bf16[512,512]{1,0:T(8,128)(2,1)}, f32[3,512]{1,0:T(4,128)}, f32[1,512]{1,0:T(1,128)}) custom-call(bf16[512,512]{1,0:T(8,128)(2,1)} %get-tuple-element.9.qg, f32[1,512]{1,0:T(1,128)} %get-tuple-element.10.loss, bf16[1024,128]{1,0:T(8,128)(2,1)} %get-tuple-element.11.land2), custom_call_target="tpu_custom_call" | custom-call | tf_op jit(solution)/shard_map/pallas_call | solution.py:550

commit v10 on v9

--- a/solution.py
+++ b/solution.py
@@ -211,24 +211,24 @@
 
     @pl.when(c == 1)
     def _():
-        pl.when(even)(functools.partial(landed, xy_own, 0))
-        pl.when(jnp.logical_not(even))(functools.partial(landed, xy_own - 1, 0))
-        unpack(xz_own, xy_own, z_at(z))
-
-        def send(pz):
-            remote(pool.at[slab_z(z)], pool.at[slab_z(z)], s2_ssem, s2_rsem.at[0], dev(x, y, pz, 1)).start()
-
-        pl.when(z != last)(functools.partial(send, last))
-        for dz in far_ring(Z):
-            pz = (z + dz) % Z
-            pl.when(pz != last)(functools.partial(send, pz))
-
         pl.when(even)(functools.partial(landed, xz_own - 1, 1))
         pl.when(jnp.logical_not(even))(functools.partial(landed, xz_own, 1))
         unpack(0, xz_own, y_at(y))
         for dy in far_ring(Y):
             remote(pool.at[slab_y(y)], pool.at[slab_y(y)],
                    s2_ssem, s2_rsem.at[1], dev(x, (y + dy) % Y, z, 1)).start()
+
+        pl.when(even)(functools.partial(landed, xy_own, 0))
+        pl.when(jnp.logical_not(even))(functools.partial(landed, xy_own - 1, 0))
+        unpack(xz_own, xy_own, z_at(z))
+
+        def send(pz):
+            remote(pool.at[slab_z(z)], pool.at[slab_z(z)], s2_ssem, s2_rsem.at[0], dev(x, y, pz, 1)).start()
+
+        pl.when(z != last)(functools.partial(send, last))
+        for dz in far_ring(Z):
+            pz = (z + dz) % Z
+            pl.when(pz != last)(functools.partial(send, pz))
 
     q_copy.wait()
     info_copy.wait()
@@ -268,7 +268,7 @@
         remote(stat.at[0, h], stat.at[1, h], pair_ssem.at[2 + h], pair_rsem.at[2 + h], partner).start()
 
     for k in range(groups):
-        g = jnp.where(c == 0, (z // 2 + near[k]) % groups, (groups // 2 + k) % groups)
+        g = jnp.where(c == 0, (z // 2 + near[k]) % groups, k)
 
         @pl.when(c == 0)
         def _():
@@ -277,9 +277,9 @@
         @pl.when(c == 1)
         def _():
             if k == 0:
+                bytes_of(pool.at[pl.ds(0, (Y - 1) * yrows)], s2_rsem.at[1]).wait()
+            if k == groups // 2:
                 bytes_of(pool.at[pl.ds(0, (Z - 1) * zrows)], s2_rsem.at[0]).wait()
-            if k == groups // 2:
-                bytes_of(pool.at[pl.ds(0, (Y - 1) * yrows)], s2_rsem.at[1]).wait()
 
         at = pl.ds(pl.multiple_of(g * tile, 16), tile)
         for i, h in enumerate(halves):

time: 48.3 us -> 49.1 us (1.017)
  Pallas kernels: 46.8 us -> 48 us
    pallas_call x1, Pallas kernels: 44.9 us -> 46.1 us  [body(): pl.pallas_call(functools.partial(kernel, X, Y, Z), out_shape=(outs[0], ou...]
where the time goes in v10:
time: 49.1 us; the launch traced here: 48.6 us
  Pallas kernels  48 us (98%)
  between operations  0.64 us (1%)
    pallas_call x1, Pallas kernels, body(): pl.pallas_call(functools.partial(kernel, X, Y, Z), out_shape=(outs[0], ou...  46.1 us
    pallas_call x1, Pallas kernels, body(): pl.pallas_call(functools.partial(finish, Y * Z, X * Z), out_shape=outs, i...  1.94 us

profile of v10, /device:TPU:1, one launch (start us, length us, event | category | flops | bytes accessed | tf_op | source)
XLA Modules:
  0.0 48.6 jit_solution(14920644422994761325)
XLA Ops:
  0.6 46.1 %shard_map.67 = (bf16[512,512]{1,0:T(8,128)(2,1)}, f32[1,512]{1,0:T(1,128)}, bf16[1024,128]{1,0:T(8,128)(2,1)}) custom-call(bf16[512,512]{1,0:T(8,128)(2,1)} %q_hbm.1, s32[1,512]{1,0:T(1,128)} %bitcast.2, s32[2]{0:T(128)} %len_hbm.1, bf16[3,512]{1,0:T(4,128)(2,1)} %it_hbm.1), custom_call_target="tpu_custom_call" | custom-call | tf_op jit(solution)/shard_map/pallas_call | solution.py:513
  46.7 1.9 %shard_map.68 = (bf16[512,512]{1,0:T(8,128)(2,1)}, f32[3,512]{1,0:T(4,128)}, f32[1,512]{1,0:T(1,128)}) custom-call(bf16[512,512]{1,0:T(8,128)(2,1)} %get-tuple-element.9.qg, f32[1,512]{1,0:T(1,128)} %get-tuple-element.10.loss, bf16[1024,128]{1,0:T(8,128)(2,1)} %get-tuple-element.11.land2), custom_call_target="tpu_custom_call" | custom-call | tf_op jit(solution)/shard_map/pallas_call | solution.py:550
